TPU v7x, 128 devices: a whole 4x4x4 slice. The times are simulated.
128 devices in a mesh: row: 8 (over y, z_hi), col: 16 (over z_lo, x, core).
Axes of the slice: x: 4, y: 4, z: 4 (z_hi: 2, z_lo: 2; z = z_hi * 2 + z_lo), core: 2. Of those that a mesh axis runs over, the one named last changes fastest.
Arguments:
- hamil: bfloat16 [4096, 4096], P('row', 'col'), as said below
- guess: bfloat16 [4096, 4096], P('row', 'col'), as said below
- pattern: int32 [64, 64], P('row', 'col'), may hold values from 0 to 1, as said below
- filters: int32 [2, 64, 64], P(None, 'row', 'col'), may hold values from 0 to 1, as said below
- deriv: bfloat16 [3, 4096, 4096], P(None, ('row', 'col')), may hold values from -6 to 6
- atom_of_row: int32 [4096], P(('row', 'col')), may hold values from 0 to 3, as said below
Outputs:
- owned_energy: bfloat16 [4096, 4096], P(('row', 'col'))
- forces: float32 [3, 512], P(None, ('row', 'col'))
Inputs may be any that keep to these rules, and one draw needn't show every extreme that they name: `atom_of_row`: within each aligned block of 32 rows (d * 32 to (d + 1) * 32 - 1) the ids never fall, begin at 0, end at 3, and every id from 0 to 3 has one row or more. Symmetric: hamil equals its transpose. Symmetric: guess equals its transpose. Symmetric 0/1 block pattern. `filters`: each step's 0/1 mask is symmetric.
All inputs are finite; a program needn't handle non-finite values.
Results may differ from a plain program's by a relative error of at most 0.04.
Values may be sent and summed in bfloat16 or wider, within the bound.
A program may use at most 64 MiB of HBM per device.

v0:
```python
import jax
import jax.numpy as jnp
from jax import lax
from jax.sharding import PartitionSpec as P

BS = 64
ATOM_DEV = 4


def expand(block_mask):
    return jnp.repeat(jnp.repeat(block_mask.astype(jnp.float32), BS, 0), BS, 1)


def columns(local_tile):
    return lax.all_gather(local_tile, "row", axis=0, tiled=True)


def fold_rows(left_tile, right_panel):
    return jnp.dot(
        lax.all_gather(left_tile, "col", axis=1, tiled=True),
        right_panel,
        preferred_element_type=jnp.float32,
    )


def body(hamil, guess, pattern, filters, deriv, atom_of_row):
    kept_mask = expand(pattern)
    rows_here, cols_here = guess.shape
    row_ids = lax.axis_index("row") * rows_here + lax.broadcasted_iota(
        jnp.int32, (rows_here, cols_here), 0
    )
    col_ids = lax.axis_index("col") * cols_here + lax.broadcasted_iota(
        jnp.int32, (rows_here, cols_here), 1
    )
    identity = jnp.where(row_ids == col_ids, 0.5, 0.0).astype(jnp.float32)
    density = (identity + guess.astype(jnp.float32)) * kept_mask
    for purify_step in range(filters.shape[0]):
        dens_bf = density.astype(jnp.bfloat16)
        right_panel = columns(dens_bf)
        square = fold_rows(dens_bf, right_panel)
        square_bf = square.astype(jnp.bfloat16)
        cube_term = fold_rows(square_bf, right_panel)
        density = expand(filters[purify_step]) * (3.0 * square - 2.0 * cube_term)
    final_bf = density.astype(jnp.bfloat16)
    ham_bf = jnp.where(kept_mask > 0, hamil, jnp.zeros_like(hamil))
    ham_dens = fold_rows(ham_bf, columns(final_bf)).astype(jnp.bfloat16)
    energy = fold_rows(final_bf, columns(ham_dens)).astype(jnp.bfloat16)
    owned_rows = lax.all_to_all(energy, "col", split_axis=0, concat_axis=1, tiled=True)
    per_row = jnp.einsum("xij,ij->xi", deriv, owned_rows, preferred_element_type=jnp.float32)
    onehot = (atom_of_row[:, None] == jnp.arange(ATOM_DEV, dtype=jnp.int32)[None, :]).astype(
        jnp.float32
    )
    forces = jnp.dot(per_row, onehot, precision=lax.Precision.HIGHEST)
    return (owned_rows, forces)


def solution(mesh):
    return jax.shard_map(
        body,
        mesh=mesh,
        in_specs=(
            P("row", "col"),
            P("row", "col"),
            P("row", "col"),
            P(None, "row", "col"),
            P(None, ("row", "col"), None),
            P(("row", "col")),
        ),
        out_specs=(P(("row", "col"), None), P(None, ("row", "col"))),
        check_vma=False,
    )
```

profile of v0, /device:TPU:1, one launch (start us, length us, event | category | flops | bytes accessed | tf_op | source)
XLA Modules:
  0.0 544.0 jit_solution(18039833839922948467)
XLA Ops:
  7.2 0.7 convert_element_type.45
  8.0 0.1 broadcast_in_dim.37
  8.0 0.1 reshape.32
  8.1 1.1 copy.12
  9.2 0.9 fusion.8
  10.1 0.0 all-gather.11.cloned.1.call-start
  10.2 0.7 all-gather.11.cloned.1.call-update
  10.9 0.0 all-gather.15.cloned.1.call-start
  10.9 59.8 %all-gather.13.cloned.1.call-done = bf16[4096,256]{0,1:T(8,128)(2,1)} async-done(((bf16[512,256]{0,1:T(8,128)(2,1)}), bf16[4096,256]{0,1:T(8,128)(2,1)}) %all-gather.13.cloned.1.call-update) | async-done | bytes 2097168 | tf_op jit(solution)/shard_map/all_gather | solution.py:15
  70.8 39.7 %all-gather.11.cloned.1.call-done = bf16[512,4096]{0,1:T(8,128)(2,1)} async-done(((bf16[512,256]{0,1:T(8,128)(2,1)}), bf16[512,4096]{0,1:T(8,128)(2,1)}) %all-gather.11.cloned.1.call-update) | async-done | bytes 4194320 | tf_op jit(solution)/shard_map/all_gather | solution.py:20
  110.5 4.9 fusion.12
  115.4 0.0 all-gather.19.cloned.1.call-start
  115.4 0.1 broadcast_in_dim.33
  115.5 0.1 reshape.30
  115.6 0.1 broadcast_in_dim.34
  115.7 0.2 copy.13
  115.9 44.6 %all-gather.15.cloned.1.call-done = bf16[512,4096]{1,0:T(8,128)(2,1)} async-done(((bf16[512,256]{1,0:T(8,128)(2,1)}), bf16[512,4096]{1,0:T(8,128)(2,1)}) %all-gather.15.cloned.1.call-update) | async-done | bytes 4194320 | tf_op jit(solution)/shard_map/all_gather | solution.py:20
  160.5 4.9 fusion.5
  165.4 0.0 all-gather.17.cloned.1.call-start
  165.4 0.5 all-gather.17.cloned.1.call-update
  166.0 52.9 %all-gather.19.cloned.1.call-done = bf16[4096,256]{1,0:T(8,128)(2,1)} async-done(((bf16[512,256]{1,0:T(8,128)(2,1)}), bf16[4096,256]{1,0:T(8,128)(2,1)}) %all-gather.19.cloned.1.call-update) | async-done | bytes 2097168 | tf_op jit(solution)/shard_map/all_gather | solution.py:15
  219.0 47.4 %all-gather.17.cloned.1.call-done = bf16[512,4096]{1,0:T(8,128)(2,1)} async-done(((bf16[512,256]{1,0:T(8,128)(2,1)}), bf16[512,4096]{1,0:T(8,128)(2,1)}) %all-gather.17.cloned.1.call-update) | async-done | bytes 4194320 | tf_op jit(solution)/shard_map/all_gather | solution.py:20
  266.4 4.8 fusion.13
  271.2 0.0 all-gather.25.cloned.1.call-start
  271.3 0.1 copy.15
  271.4 0.7 fusion.9
  272.2 0.0 all-gather.27.cloned.1.call-start
  272.3 0.1 broadcast_in_dim.31
  272.3 0.1 reshape.28
  272.4 0.1 broadcast_in_dim.32
  272.5 0.2 copy.14
  272.7 43.8 %all-gather.21.cloned.1.call-done = bf16[512,4096]{1,0:T(8,128)(2,1)} async-done(((bf16[512,256]{1,0:T(8,128)(2,1)}), bf16[512,4096]{1,0:T(8,128)(2,1)}) %all-gather.21.cloned.1.call-update) | async-done | bytes 4194320 | tf_op jit(solution)/shard_map/all_gather | solution.py:20
  316.5 4.8 fusion.4
  321.4 0.0 all-gather.29.cloned.1.call-start
  321.4 34.4 %all-gather.25.cloned.1.call-done = bf16[512,4096]{0,1:T(8,128)(2,1)} async-done(((bf16[512,256]{0,1:T(8,128)(2,1)}), bf16[512,4096]{0,1:T(8,128)(2,1)}) %all-gather.25.cloned.1.call-update) | async-done | bytes 4194320 | tf_op jit(solution)/shard_map/all_gather | solution.py:20
  355.8 56.2 %all-gather.27.cloned.1.call-done = bf16[4096,256]{1,0:T(8,128)(2,1)} async-done(((bf16[512,256]{1,0:T(8,128)(2,1)}), bf16[4096,256]{1,0:T(8,128)(2,1)}) %all-gather.27.cloned.1.call-update) | async-done | bytes 2097168 | tf_op jit(solution)/shard_map/all_gather | solution.py:15
  412.0 4.9 convolution_convert_fusion.1
  416.9 0.0 all-gather.23.cloned.1.call-start
  417.0 0.5 all-gather.23.cloned.1.call-update
  417.5 53.2 %all-gather.29.cloned.1.call-done = bf16[4096,256]{1,0:T(8,128)(2,1)} async-done(((bf16[512,256]{1,0:T(8,128)(2,1)}), bf16[4096,256]{1,0:T(8,128)(2,1)}) %all-gather.29.cloned.1.call-update) | async-done | bytes 2097168 | tf_op jit(solution)/shard_map/all_gather | solution.py:15
  470.7 47.4 %all-gather.23.cloned.1.call-done = bf16[512,4096]{1,0:T(8,128)(2,1)} async-done(((bf16[512,256]{1,0:T(8,128)(2,1)}), bf16[512,4096]{1,0:T(8,128)(2,1)}) %all-gather.23.cloned.1.call-update) | async-done | bytes 4194320 | tf_op jit(solution)/shard_map/all_gather | solution.py:20
  518.2 4.1 convolution_convert_fusion
  522.3 11.5 %all_to_all.19 = bf16[16,32,256]{2,1,0:T(8,128)(2,1)S(1)} all-to-all(bf16[16,32,256]{2,1,0:T(8,128)(2,1)S(1)} %bitcast.44), channel_id=1, replica_groups=mesh['row'=8,'col'=16] {'col'}, dimensions={0} | all-to-all | bytes 524288 | tf_op jit(solution)/shard_map/all_to_all | solution.py:48
  533.8 0.1 copy.16
  533.9 0.1 reshape.37
  534.1 0.7 copy.20
  534.8 1.6 fusion.6
  536.4 0.8 fusion.10
  (20 shorter events, 0.2 us)
Async XLA Ops:
  7.2 527.6 %copy-start = (bf16[3,32,4096]{2,1,0:T(8,128)(2,1)S(1)}, bf16[3,32,4096]{2,1,0:T(8,128)(2,1)}, u32[]{:S(2)}) copy-start(bf16[3,32,4096]{2,1,0:T(8,128)(2,1)} %param.10) | copy-start | bytes 2359300
  7.2 63.6 %all-gather.13.cloned.1.call-start = ((), (), s32[]{:S(2)}) async-start(), calls=%async_computation.2 | async-start | bytes 2359296 | tf_op jit(solution)/shard_map/all_gather | solution.py:15
  10.1 105.3 %copy-start.2 = (s32[2,8,4]{1,2,0:T(4,128)S(1)}, s32[2,8,4]{1,2,0:T(4,128)}, u32[]{:S(2)}) copy-start(s32[2,8,4]{1,2,0:T(4,128)} %param.9) | copy-start | bytes 772
  10.1 100.3 %all-gather.11.cloned.1.call-start = ((), (), s32[]{:S(2)}) async-start(), calls=%async_computation.1 | async-start | bytes 4456448 | tf_op jit(solution)/shard_map/all_gather | solution.py:20
  10.9 149.6 %all-gather.15.cloned.1.call-start = ((), (), s32[]{:S(2)}) async-start(), calls=%async_computation.3 | async-start | bytes 4456448 | tf_op jit(solution)/shard_map/all_gather | solution.py:20
  115.4 103.6 %all-gather.19.cloned.1.call-start = ((), (), s32[]{:S(2)}) async-start(), calls=%async_computation.5 | async-start | bytes 2359296 | tf_op jit(solution)/shard_map/all_gather | solution.py:15
  165.4 105.9 %copy-start.1 = (bf16[512,256]{1,0:T(8,128)(2,1)S(1)}, bf16[512,256]{1,0:T(8,128)(2,1)}, u32[]{:S(2)}) copy-start(bf16[512,256]{1,0:T(8,128)(2,1)} %param.6) | copy-start | bytes 786436
  165.4 101.0 %all-gather.17.cloned.1.call-start = ((), (), s32[]{:S(2)}) async-start(), calls=%async_computation.4 | async-start | bytes 4456448 | tf_op jit(solution)/shard_map/all_gather | solution.py:20
  166.0 150.5 %all-gather.21.cloned.1.call-start = ((), (), s32[]{:S(2)}) async-start(), calls=%async_computation.6 | async-start | bytes 4456448 | tf_op jit(solution)/shard_map/all_gather | solution.py:20
  271.2 84.6 %all-gather.25.cloned.1.call-start = ((), (), s32[]{:S(2)}) async-start(), calls=%async_computation.8 | async-start | bytes 4456448 | tf_op jit(solution)/shard_map/all_gather | solution.py:20
  272.2 139.8 %all-gather.27.cloned.1.call-start = ((), (), s32[]{:S(2)}) async-start(), calls=%async_computation.9 | async-start | bytes 2359296 | tf_op jit(solution)/shard_map/all_gather | solution.py:15
  321.4 149.4 %all-gather.29.cloned.1.call-start = ((), (), s32[]{:S(2)}) async-start(), calls=%async_computation.10 | async-start | bytes 2359296 | tf_op jit(solution)/shard_map/all_gather | solution.py:15
  416.9 101.2 %all-gather.23.cloned.1.call-start = ((), (), s32[]{:S(2)}) async-start(), calls=%async_computation.7 | async-start | bytes 4456448 | tf_op jit(solution)/shard_map/all_gather | solution.py:20
  522.3 14.1 %copy-start.3 = (s32[32]{0:T(128)S(1)}, s32[32]{0:T(128)}, u32[]{:S(2)}) copy-start(s32[32]{0:T(128)} %param.11) | copy-start | bytes 388
Sparse Core Ops, SparseCore 0:
  10.8 59.9 all-gather.12
  73.1 37.3 all-gather.10
  115.5 44.9 all-gather.14
  165.5 53.4 all-gather.18
  221.0 45.3 all-gather.16
  271.4 45.1 all-gather.20
  318.2 37.5 all-gather.24
  358.7 53.2 all-gather.26
  417.1 53.6 all-gather.28
  472.8 45.3 all-gather.22
where the time goes:
time: 544 us
  waiting for transfers between devices  482 us (89%)
  matrix products  30.7 us (6%)
  between operations  14.3 us (3%)
  blocking collectives  11.5 us (2%)
    all_gather x6, waiting for transfers between devices, fold_rows(): lax.all_gather(left_tile, 'col', axis=1, tiled=True)  257 us
    all_gather x4, waiting for transfers between devices, columns(): return lax.all_gather(local_tile, 'row', axis=0, tiled=True)  222 us
    dot_general x6, matrix products, fold_rows(): jnp.dot(lax.all_gather(left_tile, 'col', axis=1, tiled=True), right_panel...  28.4 us
    all_to_all x1, blocking collectives, body(): lax.all_to_all(energy, 'col', split_axis=0, concat_axis=1, tiled=True)  11.5 us
  transfers between devices with their start and end apart: 10, of which 10 were waited for; matrix products, arithmetic and copies ran while one was open for 1% of the time, Pallas kernels for 0%

commit v1 on v0

v1 whole, which is shorter than its diff:
```python
import functools

import jax
import jax.numpy as jnp
from jax import lax
from jax.experimental import pallas as pl
from jax.experimental.pallas import tpu as pltpu
from jax.sharding import PartitionSpec as P

MESH = pl.DeviceIdType.MESH
BS = 64
ATOM_DEV = 4
ROWS, COLS, OWN, N = 512, 256, 32, 4096
BF, F32 = jnp.bfloat16, jnp.float32


class Place:
    def __init__(self):
        self.r, self.c = lax.axis_index("row"), lax.axis_index("col")
        self.y, self.zh = self.r // 2, self.r % 2
        self.zl, self.x, self.k = self.c // 8, (self.c // 2) % 4, self.c % 2

    def col(self, dz, dx, dk=0):
        return ((self.zl + dz) % 2) * 8 + ((self.x + dx) % 4) * 2 + (self.k + dk) % 2

    def row(self, dz, dy):
        return ((self.y + dy) % 4) * 2 + (self.zh + dz) % 2

    def along(self, dz, dx, dk=0):
        return (self.r, self.col(dz, dx, dk))

    def across(self, dz, dy):
        return (self.row(dz, dy), self.c)


class Copies:
    def __init__(self, send_sems, recv_sems):
        self.send_sems, self.recv_sems = send_sems, recv_sems
        self.sent, self.n_send, self.n_recv = [], 0, 0

    def take(self, count):
        first = self.n_recv
        self.n_recv += count
        return first

    def make(self, src, dst, recv, device, send):
        return pltpu.make_async_remote_copy(
            src_ref=src,
            dst_ref=dst,
            send_sem=self.send_sems.at[send],
            recv_sem=self.recv_sems.at[recv],
            device_id=device,
            device_id_type=MESH,
        )

    def send(self, src, dst, recv, device):
        copy = self.make(src, dst, recv, device, self.n_send)
        self.n_send += 1
        copy.start()
        self.sent.append(copy)
        return copy

    def arrive(self, ref, recv, device):
        self.make(ref, ref, recv, device, 0).wait_recv()

    def drain(self, copies=None):
        for copy in list(self.sent if copies is None else copies):
            copy.wait_send()
            self.sent = [other for other in self.sent if other is not copy]


def block_cols(buf, c):
    return buf.at[:, pl.ds(pl.multiple_of(c * COLS, COLS), COLS)]


def block_rows(buf, r):
    return buf.at[pl.ds(pl.multiple_of(r * ROWS, ROWS), ROWS)]


class Gather:
    def __init__(self, cp, me, buf, axis):
        self.cp, self.me, self.buf, self.axis = cp, me, buf, axis
        self.sent = []
        self.recv = cp.take(8)
        self.side = cp.take(8) if axis == "col" else None

    def slot(self, dz, d, dk=0):
        if self.axis == "col":
            return block_cols(self.buf, self.me.col(dz, d, dk))
        return block_rows(self.buf, self.me.row(dz, d))

    def peer(self, dz, d):
        return self.me.along(dz, d) if self.axis == "col" else self.me.across(dz, d)

    def push(self, dz):
        block = self.slot(dz, 0)
        for d in (1, 3, 2):
            self.sent.append(self.cp.send(block, block, self.recv + dz * 4 + d, self.peer(0, d)))

    def share(self, dz, d):
        if self.axis == "col":
            block = self.slot(dz, -d)
            self.sent.append(self.cp.send(block, block, self.side + dz * 4 + d, self.me.along(0, 0, 1)))

    def start(self):
        block = self.slot(0, 0)
        self.sent.append(self.cp.send(block, block, self.recv + 4, self.peer(1, 0)))
        self.push(0)
        self.share(0, 0)

    def arrive(self, dz, d):
        self.cp.arrive(self.slot(dz, -d), self.recv + dz * 4 + d, self.peer(1, 0))
        self.share(dz, d)

    def forward(self):
        self.arrive(1, 0)
        self.push(1)

    def arrive_side(self, dz, d):
        self.cp.arrive(self.slot(dz, -d, 1), self.side + dz * 4 + d, self.peer(1, 0))


ORDER = [(0, 1), (0, 3), (0, 2), (1, 1), (1, 3), (1, 2)]


def gather_all(gathers):
    for g in gathers:
        g.forward()
    for dz, d in ORDER:
        for g in gathers:
            g.arrive(dz, d)


def dot(a, b):
    return jnp.dot(a, b, preferred_element_type=F32)


def mask_rows(read):
    lane = lax.broadcasted_iota(jnp.int32, (1, COLS), 1) // BS
    out = []
    for i in range(ROWS // BS):
        row = jnp.zeros((1, COLS), F32)
        for j in range(COLS // BS):
            row = jnp.where(lane == j, read(i, j).astype(F32), row)
        out.append(row)
    return out


def kernel(
    hamil, guess, pattern, filters, deriv, atoms,
    energy_out, forces_out,
    rowp, colp, srow, hcol, square, etile, eall, send_sems, recv_sems,
):
    me = Place()
    cp = Copies(send_sems, recv_sems)
    peers = [me.along(dz, dx, dk) for dz in range(2) for dx in range(4) for dk in range(2)][1:]
    peers += [me.across(0, 1), me.across(0, 2), me.across(0, 3), me.across(1, 0)]
    barrier = pltpu.get_barrier_semaphore()
    for peer in peers:
        pl.semaphore_signal(barrier, inc=1, device_id=peer, device_id_type=MESH)

    kept = mask_rows(lambda i, j: pattern[i, j])
    own_row, own_col = block_cols(rowp, me.c), block_rows(colp.at[0], me.r)
    own_ham = block_rows(hcol, me.r)
    for i in range(ROWS // BS):
        part = slice(i * BS, (i + 1) * BS)
        here = me.r * ROWS + i * BS + lax.broadcasted_iota(jnp.int32, (BS, COLS), 0)
        there = me.c * COLS + lax.broadcasted_iota(jnp.int32, (BS, COLS), 1)
        half = jnp.where(here == there, 0.5, 0.0).astype(F32)
        dens = ((half + guess[part].astype(F32)) * kept[i]).astype(BF)
        own_row[part] = dens
        own_col[part] = dens
        own_ham[part] = jnp.where(kept[i] > 0, hamil[part].astype(F32), 0.0).astype(BF)
    pl.semaphore_wait(barrier, len(peers))

    ham = None
    for step in range(3):
        panel = colp.at[step % 2]
        rows, cols = Gather(cp, me, rowp, "col"), Gather(cp, me, panel, "row")
        rows.start()
        cols.start()
        gather_all([rows, cols])
        for dz, d in [(0, 0), (1, 0)] + ORDER:
            rows.arrive_side(dz, d)
        if step == 2:
            for dz, d in ORDER:
                ham.arrive(dz, d)
        cp.drain()
        first = dot(rowp[...], hcol[...] if step == 2 else panel[...])
        own = block_cols(srow, me.c)
        own[...] = first.astype(BF)
        inner = Gather(cp, me, srow, "col")
        inner.start()
        if step == 0:
            ham = Gather(cp, me, hcol, "row")
            ham.start()
        if step < 2:
            square[...] = first
        inner.forward()
        if step == 0:
            ham.forward()
        total = None
        for dk in range(2):
            for dz, d in [(0, 0), (1, 0)] + ORDER:
                if dk == 1:
                    inner.arrive_side(dz, d)
                elif (dz, d) in ORDER:
                    inner.arrive(dz, d)
                at = pl.ds(pl.multiple_of(me.col(dz, -d, dk) * COLS, COLS), COLS)
                term = dot(srow[:, at], panel[at])
                total = term if total is None else total + term
        cp.drain(inner.sent)
        if step < 2:
            keep = mask_rows(lambda i, j: filters[step, i, j])
            after = block_rows(colp.at[(step + 1) % 2], me.r)
            for i in range(ROWS // BS):
                part = slice(i * BS, (i + 1) * BS)
                dens = (keep[i] * (3.0 * square[part] - 2.0 * total[part])).astype(BF)
                own_row[part] = dens
                after[part] = dens
        else:
            etile[...] = total.astype(BF)

    base = cp.take(16)
    mine = pl.ds(pl.multiple_of(me.c * COLS, COLS), COLS)
    rels = [(dz, dx, dk) for dx in (2, 1, 3, 0) for dz in (1, 0) for dk in range(2)]
    rels.remove((0, 0, 0))
    for dz, dx, dk in rels:
        target = me.col(dz, dx, dk)
        src = etile.at[pl.ds(pl.multiple_of(target * OWN, OWN), OWN)]
        cp.send(src, eall.at[:, mine], base + dz * 8 + dx * 2 + dk, (me.r, target))
    eall[:, mine] = etile[pl.ds(pl.multiple_of(me.c * OWN, OWN), OWN)]
    for dz, dx, dk in rels:
        cp.arrive(block_cols(eall, me.col(dz, -dx, dk)), base + dz * 8 + dx * 2 + dk, me.along(1, 0))
    energy = eall[...]
    energy_out[...] = energy
    wide = energy.astype(F32)
    line = lax.broadcasted_iota(jnp.int32, (3, ATOM_DEV), 0)
    lane = lax.broadcasted_iota(jnp.int32, (3, ATOM_DEV), 1)
    forces = jnp.zeros((3, ATOM_DEV), F32)
    for axis in range(3):
        per_row = jnp.sum(deriv[axis].astype(F32) * wide, axis=1, keepdims=True)
        for atom in range(ATOM_DEV):
            force = jnp.sum(jnp.where(atoms[...] == atom, per_row, 0.0))
            forces = jnp.where((line == axis) & (lane == atom), force, forces)
    forces_out[...] = forces
    cp.drain()


def body(hamil, guess, pattern, filters, deriv, atom_of_row):
    vmem, smem = pl.BlockSpec(memory_space=pltpu.VMEM), pl.BlockSpec(memory_space=pltpu.SMEM)
    return pl.pallas_call(
        kernel,
        out_shape=(
            jax.ShapeDtypeStruct((OWN, N), BF),
            jax.ShapeDtypeStruct((3, ATOM_DEV), F32),
        ),
        in_specs=[vmem, vmem, smem, smem, vmem, vmem],
        out_specs=(vmem, vmem),
        scratch_shapes=[
            pltpu.VMEM((ROWS, N), BF),
            pltpu.VMEM((2, N, COLS), BF),
            pltpu.VMEM((ROWS, N), BF),
            pltpu.VMEM((N, COLS), BF),
            pltpu.VMEM((ROWS, COLS), F32),
            pltpu.VMEM((ROWS, COLS), BF),
            pltpu.VMEM((OWN, N), BF),
            pltpu.SemaphoreType.DMA((160,)),
            pltpu.SemaphoreType.DMA((160,)),
        ],
        compiler_params=pltpu.CompilerParams(
            collective_id=0, has_side_effects=True, vmem_limit_bytes=48 * 1024 * 1024
        ),
    )(hamil, guess, pattern, filters, deriv, atom_of_row.reshape(OWN, 1))


def solution(mesh):
    return jax.shard_map(
        body,
        mesh=mesh,
        in_specs=(
            P("row", "col"),
            P("row", "col"),
            P("row", "col"),
            P(None, "row", "col"),
            P(None, ("row", "col"), None),
            P(("row", "col")),
        ),
        out_specs=(P(("row", "col"), None), P(None, ("row", "col"))),
        check_vma=False,
    )
```

time: 544 us -> 195 us (0.36)
  waiting for transfers between devices: 482 us -> 0 us
  Pallas kernels: 0 us -> 187 us
  matrix products: 30.7 us -> 0 us
  between operations: 14.3 us -> 0.65 us
  blocking collectives: 11.5 us -> 0 us
    all_gather x10 -> x0, waiting for transfers between devices: 480 us -> none  [the longest x6 257 us: fold_rows(): lax.all_gather(left_tile, 'col', axis=1, tiled=True)]
    pallas_call x0 -> x1, Pallas kernels: none -> 187 us  [body(): pl.pallas_call(kernel, out_shape=(jax.ShapeDtypeStruct((OWN, N), BF), jax...]
    dot_general x8 -> x0, matrix products: 30.7 us -> none  [the longest x6 28.4 us: fold_rows(): jnp.dot(lax.all_gather(left_tile, 'col', axis=1, tiled=True), right_panel...]
    all_to_all x1 -> x0, blocking collectives: 11.5 us -> none  [body(): lax.all_to_all(energy, 'col', split_axis=0, concat_axis=1, tiled=True)]
  transfers between devices with their start and end apart: 10 -> 0, of which waited for: 10 -> 0; matrix products, arithmetic and copies ran while one was open for 1% -> 0% of each run, Pallas kernels for 0% -> 0%
where the time goes in v1:
time: 195 us; the launch traced here: 194 us
  Pallas kernels  187 us (96%)
  local copies, waits for them, and re-layouts  5.82 us (3%)
    pallas_call x1, Pallas kernels, body(): pl.pallas_call(kernel, out_shape=(jax.ShapeDtypeStruct((OWN, N), BF), jax...  187 us
    unnamed x14, local copies, waits for them, and re-layouts  5.74 us

profile of v1, /device:TPU:1, one launch (start us, length us, event | category | flops | bytes accessed | tf_op | source)
XLA Modules:
  0.0 193.9 jit_solution(970799426964936534)
XLA Ops:
  0.6 0.0 copy-start.3
  0.6 0.8 copy.8.pattern
  1.4 0.0 copy-done.3
  1.4 0.0 copy-start.4
  1.4 0.1 copy.9.filters
  1.5 0.6 copy-done.4
  2.1 0.1 copy.10.atoms
  2.1 0.0 copy-start
  2.2 1.1 copy-done
  3.3 0.0 copy-start.1
  3.3 0.9 copy-done.1
  4.2 0.0 copy-start.2
  4.2 0.9 copy-done.2
  5.2 187.5 %shard_map.77 = (bf16[32,4096]{1,0:T(8,128)(2,1)S(1)}, f32[3,4]{1,0:T(4,128)S(1)}) custom-call(bf16[512,256]{1,0:T(8,128)(2,1)S(1)} %copy-done.1, bf16[512,256]{1,0:T(8,128)(2,1)S(1)} %copy-done.2, s32[8,4]{1,0:T(8,128)S(1)} %copy.8.pattern, s32[2,8,4]{2,1,0:T(8,128)S(1)} %copy.9.filters, bf16[3,32,4096]{2,1,0:T(8,128)(2,1)S(1)} %copy-done, ...), custom_call_target="tpu_custom_call" | custom-call | tf_op jit(solution)/shard_map/pallas_call | solution.py:252
  192.6 0.7 copy.13
  193.4 0.6 copy.14
Async XLA Ops:
  0.6 0.8 copy-start.3
  1.4 0.7 copy-start.4
  2.1 1.1 copy-start
  3.3 0.9 copy-start.1
  4.2 0.9 copy-start.2

commit v2 on v1

v2 whole, which is shorter than its diff:
```python
import functools

import jax
import jax.numpy as jnp
from jax import lax
from jax.experimental import pallas as pl
from jax.experimental.pallas import tpu as pltpu
from jax.sharding import PartitionSpec as P

MESH = pl.DeviceIdType.MESH
BS = 64
ATOM_DEV = 4
ROWS, COLS, OWN, N = 512, 256, 32, 4096
BF, F32 = jnp.bfloat16, jnp.float32
CHUNKS = 2
CHUNK = ROWS // CHUNKS
ORDER = [h + i for h in range(CHUNKS // 2) for i in (0, CHUNKS // 2)]


class Place:
    def __init__(self):
        self.r, self.c = lax.axis_index("row"), lax.axis_index("col")
        self.y, self.zh = self.r // 2, self.r % 2
        self.zl, self.x, self.k = self.c // 8, (self.c // 2) % 4, self.c % 2

    def col(self, dz, dx, dk=0):
        return ((self.zl + dz) % 2) * 8 + ((self.x + dx) % 4) * 2 + (self.k + dk) % 2

    def row(self, dz, dy):
        return ((self.y + dy) % 4) * 2 + (self.zh + dz) % 2

    def along(self, dz, dx, dk=0):
        return (self.r, self.col(dz, dx, dk))

    def across(self, dz, dy):
        return (self.row(dz, dy), self.c)


class Copies:
    def __init__(self, send_sems, recv_sems):
        self.send_sems, self.recv_sems = send_sems, recv_sems

    def make(self, src, dst, send, recv, device):
        return pltpu.make_async_remote_copy(
            src_ref=src,
            dst_ref=dst,
            send_sem=self.send_sems.at[send],
            recv_sem=self.recv_sems.at[recv],
            device_id=device,
            device_id_type=MESH,
        )

    def send(self, src, dst, send, recv, device):
        self.make(src, dst, send, recv, device).start()

    def arrive(self, ref, recv, device):
        self.make(ref, ref, 0, recv, device).wait_recv()

    def sent(self, ref, send, device):
        self.make(ref, ref, send, 0, device).wait_send()


def tile_cols(buf, c, lo=0, size=ROWS):
    return buf.at[lo : lo + size, pl.ds(pl.multiple_of(c * COLS, COLS), COLS)]


def tile_rows(buf, r, lo=0, size=ROWS):
    return buf.at[pl.ds(pl.multiple_of(r * ROWS + lo, size), size)]


class Gather:
    RECV = 2 * (CHUNKS + 2) + CHUNKS

    def __init__(self, cp, me, buf, axis, send, recv):
        self.cp, self.me, self.buf, self.axis = cp, me, buf, axis
        self.send, self.recv = send, recv

    def ref(self, dz, d, lo=0, size=ROWS, dk=0):
        if self.axis == "col":
            return tile_cols(self.buf, self.me.col(dz, d, dk), lo, size)
        return tile_rows(self.buf, self.me.row(dz, d), lo, size)

    def chunk(self, dz, d, h):
        return self.ref(dz, d, h * CHUNK, CHUNK)

    def peer(self, dz, d):
        return self.me.along(dz, d) if self.axis == "col" else self.me.across(dz, d)

    def put(self, ref, recv, device):
        self.cp.send(ref, ref, self.send, self.recv + recv, device)

    def got(self, ref, recv):
        self.cp.arrive(ref, self.recv + recv, self.peer(1, 0))

    def at(self, dz, d, h):
        passed = (d == 1 and h < CHUNKS // 2) or (d == 3 and h >= CHUNKS // 2)
        return CHUNKS + dz * (CHUNKS + 2) + (h if passed else CHUNKS if d != 2 else CHUNKS + 1)

    def push(self, dz, d, h):
        self.put(self.chunk(dz, 0, h), self.at(dz, d, h), self.peer(0, d))

    def pass_on(self, dz):
        for h in ORDER:
            d = 1 if h < CHUNKS // 2 else 3
            self.got(self.chunk(dz, -d, h), self.at(dz, d, h))
            self.put(self.chunk(dz, -d, h), self.at(dz, 2, h), self.peer(0, d))

    def share(self, dz, d):
        if self.axis == "col":
            self.put(self.ref(dz, -d), Gather.RECV + dz * 4 + d, self.me.along(0, 0, 1))

    def start(self):
        for h in ORDER:
            self.put(self.chunk(0, 0, h), h, self.peer(1, 0))
        for h in ORDER:
            self.push(0, 1 if h < CHUNKS // 2 else 3, h)
        for h in ORDER:
            self.push(0, 3 if h < CHUNKS // 2 else 1, h)
        self.share(0, 0)

    def push_partner(self):
        for h in ORDER:
            self.got(self.chunk(1, 0, h), h)
            self.push(1, 1 if h < CHUNKS // 2 else 3, h)
        for h in ORDER:
            self.push(1, 3 if h < CHUNKS // 2 else 1, h)
        self.share(1, 0)

    def near(self, dz):
        self.got(self.ref(dz, 0), self.at(dz, 1, CHUNKS - 1))
        self.share(dz, 1)
        self.share(dz, 3)

    def far(self, dz):
        self.got(self.ref(dz, 2), self.at(dz, 2, 0))
        self.share(dz, 2)

    def shared(self, dz, d):
        self.got(self.ref(dz, -d, dk=1), Gather.RECV + dz * 4 + d)

    def drain(self):
        count = 7 + (8 if self.axis == "col" else 0)
        if self.axis == "col":
            whole = self.buf.at[:, : count * COLS]
        else:
            whole = self.buf.at[: count * ROWS]
        self.cp.sent(whole, self.send, self.peer(1, 0))


PARTS = [
    lambda g: g.start(),
    lambda g: g.pass_on(0),
    lambda g: g.push_partner(),
    lambda g: g.near(0),
    lambda g: g.pass_on(1),
    lambda g: g.far(0),
    lambda g: g.near(1),
    lambda g: g.far(1),
]
TILES = [(dz, d) for dz in range(2) for d in (0, 1, 3, 2)]


def dot(a, b):
    return jnp.dot(a, b, preferred_element_type=F32)


def mask_rows(blocks):
    lane = lax.broadcasted_iota(jnp.int32, (1, COLS), 1) // BS
    blocks = blocks.astype(F32)
    out = []
    for i in range(ROWS // BS):
        row = jnp.zeros((1, COLS), F32)
        for j in range(COLS // BS):
            row = jnp.where(lane == j, blocks[i : i + 1, j : j + 1], row)
        out.append(row)
    return out


def kernel(
    hamil_hbm, guess_hbm, pattern_hbm, filters_hbm, deriv_hbm, atoms_hbm,
    energy_out, forces_out,
    hamil, guess, pattern, filters, deriv, atoms,
    rowp, colp, srow, hcol, square, etile, eall, load_sems, send_sems, recv_sems,
):
    me = Place()
    cp = Copies(send_sems, recv_sems)
    peers = [me.along(dz, dx, dk) for dz in range(2) for dx in range(4) for dk in range(2)][1:]
    peers += [me.across(0, 1), me.across(0, 2), me.across(0, 3), me.across(1, 0)]
    barrier = pltpu.get_barrier_semaphore()
    for peer in peers:
        pl.semaphore_signal(barrier, inc=1, device_id=peer, device_id_type=MESH)

    pairs = [(pattern_hbm, pattern), (guess_hbm, guess), (hamil_hbm, hamil)]
    pairs += [(filters_hbm, filters), (deriv_hbm, deriv), (atoms_hbm, atoms)]
    loads = [pltpu.make_async_copy(a, b, load_sems.at[i]) for i, (a, b) in enumerate(pairs)]
    for load in loads:
        load.start()
    for load in loads[:3]:
        load.wait()

    kept = mask_rows(pattern[...])
    own_row = tile_cols(rowp, me.c)
    own_col = [tile_rows(colp.at[i], me.r) for i in range(2)]
    own_ham = tile_rows(hcol, me.r)
    for i in range(ROWS // BS):
        part = slice(i * BS, (i + 1) * BS)
        here = me.r * ROWS + i * BS + lax.broadcasted_iota(jnp.int32, (BS, COLS), 0)
        there = me.c * COLS + lax.broadcasted_iota(jnp.int32, (BS, COLS), 1)
        half = jnp.where(here == there, 0.5, 0.0).astype(F32)
        dens = ((half + guess[part].astype(F32)) * kept[i]).astype(BF)
        own_row[part] = dens
        own_col[0][part] = dens
        own_ham[part] = jnp.where(kept[i] > 0, hamil[part].astype(F32), 0.0).astype(BF)
    pl.semaphore_wait(barrier, len(peers))

    step_sems = Gather.RECV + 8
    for step in range(3):
        panel = colp.at[step % 2]
        rows = Gather(cp, me, rowp, "col", 0, 0)
        inner = Gather(cp, me, srow, "col", 1, step_sems)
        cols = Gather(cp, me, panel, "row", 2 + step % 2, 2 * step_sems + step % 2 * Gather.RECV)
        ham = Gather(cp, me, hcol, "row", 4, 2 * step_sems + 2 * Gather.RECV)
        for part in PARTS:
            part(rows)
            part(cols)
        for dz, d in TILES:
            rows.shared(dz, d)
        rows.drain()
        cols.drain()
        first = dot(rowp[...], hcol[...] if step == 2 else panel[...])
        tile_cols(srow, me.c)[...] = first.astype(BF)

        total = None

        def add(dk, *tiles):
            nonlocal total
            for dz, d in tiles:
                if dk:
                    inner.shared(dz, d)
                at = pl.ds(pl.multiple_of(me.col(dz, -d, dk) * COLS, COLS), COLS)
                term = dot(srow[:, at], panel[at])
                total = term if total is None else total + term

        for i, part in enumerate(PARTS):
            part(inner)
            if step == 0:
                part(ham)
            if i == 0:
                if step < 2:
                    square[...] = first
                add(0, (0, 0))
            if i == 2:
                add(1, (0, 0))
            if i == 4:
                add(0, (0, 1), (0, 3), (1, 0))
            if i == 5:
                add(1, (0, 1), (0, 3), (1, 0))
            if i == 6:
                add(0, (0, 2), (1, 1), (1, 3))
                add(1, (0, 2))
            if i == 7:
                add(1, (1, 1), (1, 3))
                add(0, (1, 2))
                add(1, (1, 2))
        inner.drain()
        if step == 0:
            ham.drain()
        if step < 2:
            if step == 0:
                loads[3].wait()
            keep = mask_rows(filters[step])
            for i in range(ROWS // BS):
                part = slice(i * BS, (i + 1) * BS)
                dens = (keep[i] * (3.0 * square[part] - 2.0 * total[part])).astype(BF)
                own_row[part] = dens
                own_col[(step + 1) % 2][part] = dens
        else:
            etile[...] = total.astype(BF)

    out_sem = 2 * step_sems + 3 * Gather.RECV
    rels = [(dz, dx, dk) for dx in (2, 1, 3, 0) for dz in (1, 0) for dk in range(2)]
    rels.remove((0, 0, 0))
    for dz, dx, dk in rels:
        target = me.col(dz, dx, dk)
        src = etile.at[pl.ds(pl.multiple_of(target * OWN, OWN), OWN)]
        cp.send(src, tile_cols(eall, me.c, 0, OWN), 5, out_sem, (me.r, target))
    tile_cols(eall, me.c, 0, OWN)[...] = etile[pl.ds(pl.multiple_of(me.c * OWN, OWN), OWN)]
    others = eall.at[:, : len(rels) * COLS]
    cp.arrive(others, out_sem, me.along(1, 0))
    cp.sent(others, 5, me.along(1, 0))
    loads[4].wait()
    loads[5].wait()
    energy = eall[...]
    energy_out[...] = energy
    wide = energy.astype(F32)
    line = lax.broadcasted_iota(jnp.int32, (3, ATOM_DEV), 0)
    lane = lax.broadcasted_iota(jnp.int32, (3, ATOM_DEV), 1)
    forces = jnp.zeros((3, ATOM_DEV), F32)
    for axis in range(3):
        per_row = jnp.sum(deriv[axis].astype(F32) * wide, axis=1, keepdims=True)
        for atom in range(ATOM_DEV):
            force = jnp.sum(jnp.where(atoms[...] == atom, per_row, 0.0))
            forces = jnp.where((line == axis) & (lane == atom), force, forces)
    forces_out[...] = forces


def body(hamil, guess, pattern, filters, deriv, atom_of_row):
    args = (hamil, guess, pattern, filters, deriv, atom_of_row.reshape(OWN, 1))
    vmem = pl.BlockSpec(memory_space=pltpu.VMEM)
    return pl.pallas_call(
        kernel,
        out_shape=(
            jax.ShapeDtypeStruct((OWN, N), BF),
            jax.ShapeDtypeStruct((3, ATOM_DEV), F32),
        ),
        in_specs=[pl.BlockSpec(memory_space=pl.ANY)] * 6,
        out_specs=(vmem, vmem),
        scratch_shapes=[pltpu.VMEM(arg.shape, arg.dtype) for arg in args]
        + [
            pltpu.VMEM((ROWS, N), BF),
            pltpu.VMEM((2, N, COLS), BF),
            pltpu.VMEM((ROWS, N), BF),
            pltpu.VMEM((N, COLS), BF),
            pltpu.VMEM((ROWS, COLS), F32),
            pltpu.VMEM((ROWS, COLS), BF),
            pltpu.VMEM((OWN, N), BF),
            pltpu.SemaphoreType.DMA((6,)),
            pltpu.SemaphoreType.DMA((6,)),
            pltpu.SemaphoreType.DMA((2 * (Gather.RECV + 8) + 3 * Gather.RECV + 1,)),
        ],
        compiler_params=pltpu.CompilerParams(
            collective_id=0, has_side_effects=True, vmem_limit_bytes=48 * 1024 * 1024
        ),
    )(*args)


def solution(mesh):
    return jax.shard_map(
        body,
        mesh=mesh,
        in_specs=(
            P("row", "col"),
            P("row", "col"),
            P("row", "col"),
            P(None, "row", "col"),
            P(None, ("row", "col"), None),
            P(("row", "col")),
        ),
        out_specs=(P(("row", "col"), None), P(None, ("row", "col"))),
        check_vma=False,
    )
```

time: 195 us -> 164 us (0.84)
  Pallas kernels: 187 us -> 157 us
    pallas_call x1, Pallas kernels: 187 us -> 157 us  [body(): pl.pallas_call(kernel, out_shape=(jax.ShapeDtypeStruct((OWN, N), BF), jax...]
where the time goes in v2:
time: 164 us
  Pallas kernels  157 us (96%)
  local copies, waits for them, and re-layouts  5.82 us (4%)
    pallas_call x1, Pallas kernels, body(): pl.pallas_call(kernel, out_shape=(jax.ShapeDtypeStruct((OWN, N), BF), jax...  157 us
    unnamed x14, local copies, waits for them, and re-layouts  5.74 us

profile of v2, /device:TPU:1, one launch (start us, length us, event | category | flops | bytes accessed | tf_op | source)
XLA Modules:
  0.0 163.9 jit_solution(11176001880734682463)
XLA Ops:
  0.6 0.0 copy-start.3
  0.6 0.8 copy.8.pattern_hbm
  1.4 0.0 copy-done.3
  1.4 0.0 copy-start.4
  1.4 0.1 copy.9.filters_hbm
  1.5 0.6 copy-done.4
  2.1 0.1 copy.10.atoms_hbm
  2.1 0.0 copy-start
  2.2 1.1 copy-done
  3.3 0.0 copy-start.1
  3.3 0.9 copy-done.1
  4.2 0.0 copy-start.2
  4.2 0.9 copy-done.2
  5.2 157.4 %shard_map.77 = (bf16[32,4096]{1,0:T(8,128)(2,1)S(1)}, f32[3,4]{1,0:T(4,128)S(1)}) custom-call(bf16[512,256]{1,0:T(8,128)(2,1)S(1)} %copy-done.1, bf16[512,256]{1,0:T(8,128)(2,1)S(1)} %copy-done.2, s32[8,4]{1,0:T(8,128)S(1)} %copy.8.pattern_hbm, s32[2,8,4]{2,1,0:T(8,128)S(1)} %copy.9.filters_hbm, bf16[3,32,4096]{2,1,0:T(8,128)(2,1)S(1)} %copy-done, ...), custom_call_target="tpu_custom_call" | custom-call | tf_op jit(solution)/shard_map/pallas_call | solution.py:310
  162.6 0.7 copy.13
  163.3 0.6 copy.14
Async XLA Ops:
  0.6 0.8 copy-start.3
  1.4 0.7 copy-start.4
  2.1 1.1 copy-start
  3.3 0.9 copy-start.1
  4.2 0.9 copy-start.2

commit v3 on v0

v3 whole, which is shorter than its diff:
```python
import jax
import jax.numpy as jnp
from jax import lax
from jax.experimental import pallas as pl
from jax.experimental.pallas import tpu as pltpu
from jax.sharding import PartitionSpec as P

MESH = pl.DeviceIdType.MESH
BF, F32 = jnp.bfloat16, jnp.float32
BS = 64
ATOM_DEV = 4
N, OWN = 4096, 32
TALL, SLIM = 512, 256
ROWS, WIDE = 256, 512
PLANE, ROW = 16, 8


class Place:
    def __init__(self):
        row, col = lax.axis_index("row"), lax.axis_index("col")
        self.row, self.col = row, col
        self.zl = col // 8
        self.x, self.y, self.z, self.k = (col // 2) % 4, row // 2, (row % 2) * 2 + col // 8, col % 2
        self.own = self.x * 2 + self.k

    def at(self, x, y, z, k):
        return (y * 2 + z // 2, (z % 2) * 8 + x * 2 + k)

    def by(self, dx=0, dy=0, dz=0, dk=0):
        return self.at((self.x + dx) % 4, (self.y + dy) % 4, (self.z + dz) % 4, (self.k + dk) % 2)

    def partner(self):
        return (self.row, (self.col + 8) % 16)

    def line(self, dx, dk=0):
        return (self.x + dx) % 4 * 2 + (self.k + dk) % 2


class Copies:
    def __init__(self, me, send_sems, recv_sems):
        self.send_sems, self.recv_sems, self.any = send_sems, recv_sems, me.by(dx=1)

    def make(self, src, dst, send, recv, device):
        return pltpu.make_async_remote_copy(
            src_ref=src,
            dst_ref=dst,
            send_sem=self.send_sems.at[send],
            recv_sem=self.recv_sems.at[recv],
            device_id=device,
            device_id_type=MESH,
        )

    def send(self, src, dst, send, recv, device):
        self.make(src, dst, send, recv, device).start()

    def arrive(self, ref, recv):
        self.make(ref, ref, 0, recv, self.any).wait_recv()

    def sent(self, ref, send):
        self.make(ref, ref, send, 0, self.any).wait_send()


def new_piece(buf):
    def piece(y, z, t, lo, size):
        start = (y * 4 + z) * ROWS + t * (ROWS // 2) + lo
        return buf.at[pl.ds(pl.multiple_of(start, 64), size)]

    return piece


def old_piece(buf, first, rows):
    def piece(y, z, t, lo, size):
        start = (y * 2 + z // 2) * TALL + first + t * rows + lo
        return buf.at[
            pl.ds(pl.multiple_of(start, 64), size), pl.ds(pl.multiple_of(z % 2 * SLIM, SLIM), SLIM)
        ]

    return piece


class Plane:
    def __init__(self, cp, me, buf, piece, rows, width, send, recv):
        self.cp, self.me, self.buf, self.piece = cp, me, buf, piece
        self.rows, self.send, self.recv = rows, send, recv
        self.equal = rows * width // WIDE

    def ref(self, t, i, j, lo=0, size=None):
        back = (i, j) if t == 0 else (j, i)
        y, z = (self.me.y + 4 - back[0]) % 4, (self.me.z + 4 - back[1]) % 4
        return self.piece(y, z, t, lo, self.rows if size is None else size)

    def put(self, t, i, j, axis, d, sem, lo=0, size=None):
        ref = self.ref(t, i, j, lo, size)
        device = self.me.by(dy=d) if axis == t else self.me.by(dz=d)
        self.cp.send(ref, ref, self.send, self.recv + sem, device)

    def got(self, sem, pieces=1):
        self.cp.arrive(self.buf.at[: pieces * self.equal], self.recv + sem)

    def start(self):
        for t in range(2):
            self.put(t, 0, 0, 0, 1, 7 * t)
            self.put(t, 0, 0, 0, 3, 7 * t + 1)
        for t in range(2):
            self.put(t, 0, 0, 1, 1, 7 * t + 3)
            self.put(t, 0, 0, 1, 3, 7 * t + 3)

    def first_ring(self):
        half = self.rows // 2
        for t in range(2):
            self.got(7 * t)
            self.put(t, 1, 0, 0, 1, 7 * t + 2, 0, half)
            self.got(7 * t + 1)
            self.put(t, 3, 0, 0, 3, 7 * t + 2, half, half)
        for t in range(2):
            self.put(t, 1, 0, 1, 1, 14)
            self.put(t, 1, 0, 1, 3, 7 * t + 4)
            self.put(t, 3, 0, 1, 1, 7 * t + 5)
            self.put(t, 3, 0, 1, 3, 14)

    def second_own(self):
        for t in range(2):
            self.got(7 * t + 3, 2)
            self.put(t, 0, 1, 1, 1, 15)

    def first_far(self):
        for t in range(2):
            self.got(7 * t + 2)
            self.put(t, 2, 0, 1, 1, 14)
            self.put(t, 2, 0, 1, 3, 7 * t + 6)

    def second_left(self):
        for t in range(2):
            self.got(7 * t + 4)
            self.put(t, 1, 3, 1, 3, 15)

    def second_right(self):
        for t in range(2):
            self.got(7 * t + 5)
            self.put(t, 3, 1, 1, 1, 15)

    def second_far(self):
        for t in range(2):
            self.got(7 * t + 6)
            self.put(t, 2, 3, 1, 3, 15)

    def near(self):
        self.got(14, 6)

    def far(self):
        self.got(15, 8)

    def drain(self):
        self.cp.sent(self.buf.at[: 30 * self.equal], self.send)


class Row:
    def __init__(self, cp, me, buf, send, recv):
        self.cp, self.me, self.buf, self.send, self.recv = cp, me, buf, send, recv

    def ref(self, d, dk=0, lo=0, size=ROWS):
        at = pl.multiple_of(self.me.line(4 - d, dk) * WIDE, WIDE)
        return self.buf.at[lo : lo + size, pl.ds(at, WIDE)]

    def put(self, d, to, sem, half=None, dk=0):
        ref = self.ref(d) if half is None else self.ref(d, 0, half * (ROWS // 2), ROWS // 2)
        self.cp.send(ref, ref, self.send, self.recv + sem, self.me.by(dx=to, dk=dk))

    def got(self, sem):
        self.cp.arrive(self.ref(0), self.recv + sem)

    def got_half(self, sem):
        self.cp.arrive(self.ref(0, 0, 0, ROWS // 2), self.recv + sem)

    def share(self, d):
        self.put(d, 0, 4 + d, dk=1)

    def start(self):
        self.put(0, 1, 0, 0)
        self.put(0, 3, 1, 1)
        self.put(0, 1, 2, 1)
        self.put(0, 3, 2, 0)
        self.share(0)

    def pass_on(self):
        self.got_half(0)
        self.put(1, 1, 3, 0)
        self.got_half(1)
        self.put(3, 3, 3, 1)

    def near(self):
        self.got(2)
        self.share(1)
        self.share(3)

    def far(self):
        self.got(3)
        self.share(2)

    def shared(self, *tiles):
        for d in tiles:
            self.got(4 + d)

    def drain(self):
        self.cp.sent(self.buf.at[:, : 7 * WIDE], self.send)


def dot(a, b):
    return jnp.dot(a, b, preferred_element_type=F32)


def block_k(b, zl):
    return pl.ds(pl.multiple_of((zl * 8 + b) * ROWS, ROWS), ROWS)


class Product:
    def __init__(self, left, right):
        self.left, self.right, self.total = left, right, None

    def add(self, b, zl):
        at = pl.ds(pl.multiple_of(b * WIDE + zl * SLIM, SLIM), SLIM)
        term = dot(self.left[:, at], self.right[block_k(b, zl)])
        self.total = term if self.total is None else self.total + term

    def tiles(self, me, dk, *ds):
        for d in ds:
            for zl in range(2):
                self.add(me.line(4 - d, dk), zl)


def mask_row(blocks, i):
    count = blocks.shape[0]
    lane = lax.broadcasted_iota(jnp.int32, (1, count * BS), 1) // BS
    row = jnp.zeros((1, count * BS), F32)
    for j in range(count):
        row = jnp.where(lane == j, blocks[j : j + 1, i : i + 1], row)
    return row


def kernel(
    hamil_hbm, guess_hbm, pattern_hbm, filters_hbm, deriv_hbm, atoms_hbm,
    energy_out, forces_out,
    hamil, guess, pattern, filters, deriv, atoms,
    rowp, colp, srow, hcol, square, etile, eall, others, load_sems, send_sems, recv_sems,
):
    me = Place()
    cp = Copies(me, send_sems, recv_sems)
    peers = [me.by(dx=dx, dk=dk) for dx in range(4) for dk in range(2)][1:]
    peers += [me.by(dy=1), me.by(dy=3), me.by(dz=1), me.by(dz=3)]
    barrier = pltpu.get_barrier_semaphore()
    for peer in peers:
        pl.semaphore_signal(barrier, inc=1, device_id=peer, device_id_type=MESH)

    pairs = [(pattern_hbm, pattern), (guess_hbm, guess), (hamil_hbm, hamil)]
    pairs += [(filters_hbm, filters), (deriv_hbm, deriv), (atoms_hbm, atoms)]
    loads = [pltpu.make_async_copy(a, b, load_sems.at[i]) for i, (a, b) in enumerate(pairs)]
    for load in loads:
        load.start()
    for load in loads[:4]:
        load.wait()

    tall = pl.ds(pl.multiple_of(me.row * TALL, TALL), TALL)
    slim = pl.ds(pl.multiple_of(me.zl * SLIM, SLIM), SLIM)
    own_guess, own_ham = colp.at[0].at[tall, slim], hcol.at[tall, slim]
    kept = pattern[...].astype(F32)
    for i in range(TALL // BS):
        part = slice(i * BS, (i + 1) * BS)
        keep = mask_row(kept, i)
        here = me.row * TALL + i * BS + lax.broadcasted_iota(jnp.int32, (BS, SLIM), 0)
        there = me.col * SLIM + lax.broadcasted_iota(jnp.int32, (BS, SLIM), 1)
        half = jnp.where(here == there, 0.5, 0.0).astype(F32)
        own_guess[part] = ((half + guess[part].astype(F32)) * keep).astype(BF)
        own_ham[part] = jnp.where(keep > 0, hamil[part].astype(F32), 0.0).astype(BF)
    pl.semaphore_wait(barrier, len(peers))

    mine = pl.ds(pl.multiple_of((me.y * 4 + me.z) * ROWS, ROWS), ROWS)
    own_rows = pl.ds(pl.multiple_of(me.own * WIDE, WIDE), WIDE)
    planes = 2 * ROW
    filters_sem, energy_sem = planes + 4 * PLANE, planes + 4 * PLANE + 1

    def early(product):
        for dy in (0, 1, 3):
            for dz in (0, 1, 3):
                add_block(product, dy, dz)

    def late(product):
        for d in range(4):
            add_block(product, d, 2)
        for d in (0, 1, 3):
            add_block(product, 2, d)

    def add_block(product, dy, dz):
        r = (me.y + 4 - dy) % 4 * 4 + (me.z + 4 - dz) % 4
        product.add(r % 8, r // 8)

    cp.send(filters, others, 6, filters_sem, me.partner())
    for step in range(3):
        panel = colp.at[step % 2]
        piece = old_piece(panel, 0, TALL // 2) if step == 0 else new_piece(panel)
        shape = (TALL // 2, SLIM) if step == 0 else (ROWS // 2, WIDE)
        plane = Plane(cp, me, panel, piece, *shape, 2 + step % 2, planes + step % 2 * PLANE)
        rows = Row(cp, me, rowp, 0, 0)
        inner = Row(cp, me, srow, 1, ROW)
        second = Product(srow, panel)
        if step < 2:
            first = Product(rowp, panel)
            plane.start()
            if step == 0:
                plane.first_ring()
                plane.second_own()
                rowp[:, own_rows] = panel[mine]
                rows.start()
                plane.first_far()
                plane.second_left()
                plane.second_right()
                rows.pass_on()
                rows.near()
                plane.second_far()
                rows.far()
            else:
                rows.start()
                plane.first_ring()
                rows.pass_on()
                plane.second_own()
                rows.near()
                plane.first_far()
                rows.far()
                plane.second_left()
                plane.second_right()
                plane.second_far()
            rows.shared(0, 1, 3, 2)
            plane.near()
            if step == 1:
                early(first)
            plane.far()
            if step == 0:
                early(first)
            late(first)
            rows.drain()
            plane.drain()
            srow[:, own_rows] = first.total.astype(BF)
            ham_piece = old_piece(hcol, step * (TALL // 2), TALL // 4)
            ham = Plane(cp, me, hcol, ham_piece, TALL // 4, SLIM, 4 + step, planes + (2 + step) * PLANE)
            inner.start()
            ham.start()
            square[...] = first.total
            second.tiles(me, 0, 0)
            ham.first_ring()
            inner.pass_on()
            ham.second_own()
            ham.first_far()
            inner.shared(0)
            second.tiles(me, 1, 0)
            inner.near()
            second.tiles(me, 0, 1, 3)
            ham.second_left()
            inner.far()
            ham.second_right()
            inner.shared(1, 3)
            second.tiles(me, 1, 1, 3)
            second.tiles(me, 0, 2)
            ham.second_far()
            inner.shared(2)
            second.tiles(me, 1, 2)
            inner.drain()
            if step == 0:
                cp.arrive(others, filters_sem)
            blocks = [filters[step].astype(F32), others[step].astype(F32)]
            keep = [jnp.where(me.zl == 0, m[:, :4], m[:, 4:]) for m in blocks]
            left = jnp.where(me.zl == 0, keep[0], keep[1])
            right = jnp.where(me.zl == 0, keep[1], keep[0])
            after = colp.at[(step + 1) % 2]
            own_piece = after.at[mine]
            own_block = rowp.at[:, own_rows]
            for i in range(ROWS // BS):
                part = slice(i * BS, (i + 1) * BS)
                mask = jnp.concatenate([mask_row(left, i), mask_row(right, i)], axis=1)
                dens = (mask * (3.0 * square[part] - 2.0 * second.total[part])).astype(BF)
                own_piece[part] = dens
                own_block[part] = dens
            ham.near()
            ham.far()
            ham.drain()
        else:
            first = Product(rowp, hcol)
            rows.start()
            plane.start()
            rows.pass_on()
            plane.first_ring()
            first.tiles(me, 0, 0)
            rows.shared(0)
            first.tiles(me, 1, 0)
            plane.second_own()
            rows.near()
            first.tiles(me, 0, 1, 3)
            plane.first_far()
            rows.far()
            rows.shared(1, 3)
            first.tiles(me, 1, 1, 3)
            first.tiles(me, 0, 2)
            plane.second_left()
            rows.shared(2)
            first.tiles(me, 1, 2)
            srow[:, own_rows] = first.total.astype(BF)
            inner.start()
            plane.second_right()
            plane.second_far()
            inner.pass_on()
            plane.near()
            inner.near()
            plane.far()
            second.tiles(me, 0, 0, 1, 3)
            inner.shared(0)
            second.tiles(me, 1, 0)
            inner.far()
            inner.shared(1, 3)
            second.tiles(me, 1, 1, 3)
            second.tiles(me, 0, 2)
            inner.shared(2)
            second.tiles(me, 1, 2)
            etile[...] = second.total.astype(BF)
            rows.drain()
            plane.drain()
            inner.drain()

    rels = [(dx, dk) for dx in (2, 1, 3, 0) for dk in range(2)][:-2] + [(0, 1)]
    for dx, dk in rels:
        src = etile.at[pl.ds(pl.multiple_of(me.line(dx, dk) * OWN, OWN), OWN)]
        cp.send(src, eall.at[:, own_rows], 0, energy_sem, me.by(dx=dx, dk=dk))
    eall[:, own_rows] = etile[pl.ds(pl.multiple_of(me.own * OWN, OWN), OWN)]
    same = lax.broadcasted_iota(jnp.int32, (OWN, OWN), 0) == lax.broadcasted_iota(jnp.int32, (OWN, OWN), 1)
    loads[4].wait()
    loads[5].wait()
    atom_of = jnp.sum(jnp.where(same, atoms[...].astype(F32), 0.0), axis=1, keepdims=True)
    cp.sent(filters, 6)
    cp.arrive(eall.at[:, : 7 * WIDE], energy_sem)
    for b in range(8):
        for zl in range(2):
            energy_out[:, (zl * 8 + b) * SLIM : (zl * 8 + b + 1) * SLIM] = eall[
                :, b * WIDE + zl * SLIM : b * WIDE + (zl + 1) * SLIM
            ]
    wide = energy_out[...].astype(F32)
    line = lax.broadcasted_iota(jnp.int32, (3, ATOM_DEV), 0)
    lane = lax.broadcasted_iota(jnp.int32, (3, ATOM_DEV), 1)
    forces = jnp.zeros((3, ATOM_DEV), F32)
    for axis in range(3):
        per_row = jnp.sum(deriv[axis].astype(F32) * wide, axis=1, keepdims=True)
        for atom in range(ATOM_DEV):
            force = jnp.sum(jnp.where(atom_of == atom, per_row, 0.0))
            forces = jnp.where((line == axis) & (lane == atom), force, forces)
    forces_out[...] = forces
    cp.sent(eall.at[:, : 7 * WIDE], 0)


def body(hamil, guess, pattern, filters, deriv, atom_of_row):
    args = (hamil, guess, pattern.T, filters.transpose(0, 2, 1), deriv, atom_of_row.reshape(1, OWN))
    vmem = pl.BlockSpec(memory_space=pltpu.VMEM)
    return pl.pallas_call(
        kernel,
        out_shape=(
            jax.ShapeDtypeStruct((OWN, N), BF),
            jax.ShapeDtypeStruct((3, ATOM_DEV), F32),
        ),
        in_specs=[pl.BlockSpec(memory_space=pl.ANY)] * 6,
        out_specs=(vmem, vmem),
        scratch_shapes=[pltpu.VMEM(arg.shape, arg.dtype) for arg in args]
        + [
            pltpu.VMEM((ROWS, N), BF),
            pltpu.VMEM((2, N, WIDE), BF),
            pltpu.VMEM((ROWS, N), BF),
            pltpu.VMEM((N, WIDE), BF),
            pltpu.VMEM((ROWS, WIDE), F32),
            pltpu.VMEM((ROWS, WIDE), BF),
            pltpu.VMEM((OWN, N), BF),
            pltpu.VMEM(args[3].shape, args[3].dtype),
            pltpu.SemaphoreType.DMA((6,)),
            pltpu.SemaphoreType.DMA((7,)),
            pltpu.SemaphoreType.DMA((2 * ROW + 4 * PLANE + 2,)),
        ],
        compiler_params=pltpu.CompilerParams(
            collective_id=0, has_side_effects=True, vmem_limit_bytes=60 * 1024 * 1024
        ),
    )(*args)


def solution(mesh):
    return jax.shard_map(
        body,
        mesh=mesh,
        in_specs=(
            P("row", "col"),
            P("row", "col"),
            P("row", "col"),
            P(None, "row", "col"),
            P(None, ("row", "col"), None),
            P(("row", "col")),
        ),
        out_specs=(P(("row", "col"), None), P(None, ("row", "col"))),
        check_vma=False,
    )
```

time: 544 us -> 122 us (0.22)
  waiting for transfers between devices: 482 us -> 0 us
  Pallas kernels: 0 us -> 119 us
  matrix products: 30.7 us -> 0 us
  between operations: 14.3 us -> 0.65 us
  blocking collectives: 11.5 us -> 0 us
    all_gather x10 -> x0, waiting for transfers between devices: 480 us -> none  [the longest x6 257 us: fold_rows(): lax.all_gather(left_tile, 'col', axis=1, tiled=True)]
    pallas_call x0 -> x1, Pallas kernels: none -> 119 us  [body(): pl.pallas_call(kernel, out_shape=(jax.ShapeDtypeStruct((OWN, N), BF), jax...]
    dot_general x8 -> x0, matrix products: 30.7 us -> none  [the longest x6 28.4 us: fold_rows(): jnp.dot(lax.all_gather(left_tile, 'col', axis=1, tiled=True), right_panel...]
    all_to_all x1 -> x0, blocking collectives: 11.5 us -> none  [body(): lax.all_to_all(energy, 'col', split_axis=0, concat_axis=1, tiled=True)]
  transfers between devices with their start and end apart: 10 -> 0, of which waited for: 10 -> 0; matrix products, arithmetic and copies ran while one was open for 1% -> 0% of each run, Pallas kernels for 0% -> 0%
where the time goes in v3:
time: 122 us
  Pallas kernels  119 us (98%)
  local copies, waits for them, and re-layouts  2.25 us (2%)
    pallas_call x1, Pallas kernels, body(): pl.pallas_call(kernel, out_shape=(jax.ShapeDtypeStruct((OWN, N), BF), jax...  119 us

profile of v3, /device:TPU:1, one launch (start us, length us, event | category | flops | bytes accessed | tf_op | source)
XLA Modules:
  0.0 122.2 jit_solution(7427323471778905885)
XLA Ops:
  0.6 119.3 %shard_map.77 = (bf16[32,4096]{1,0:T(8,128)(2,1)}, f32[3,4]{1,0:T(4,128)}) custom-call(bf16[512,256]{1,0:T(8,128)(2,1)} %hamil_hbm.1, bf16[512,256]{1,0:T(8,128)(2,1)} %guess_hbm.1, s32[4,8]{1,0:T(4,128)} %bitcast.4, s32[2,4,8]{2,1,0:T(4,128)} %bitcast.3, bf16[3,32,4096]{2,1,0:T(8,128)(2,1)} %deriv_hbm.1, s32[1,32]{1,0:T(1,128)} %bitcast.5), custom_call_target="tpu_custom_call" | custom-call | tf_op jit(solution)/shard_map/pallas_call | solution.py:458
  120.0 0.0 copy-start
  120.0 1.7 %copy.10 = bf16[32,4096]{1,0:T(8,128)(2,1)} copy(bf16[32,4096]{1,0:T(8,128)(2,1)} %get-tuple-element.4) | data formatting | bytes 524288
  121.6 0.0 copy-done
  121.6 0.6 copy.11
Async XLA Ops:
  120.0 1.7 %copy-start = (f32[3,4]{1,0:T(4,128)S(1)}, f32[3,4]{1,0:T(4,128)}, u32[]{:S(2)}) copy-start(f32[3,4]{1,0:T(4,128)} %get-tuple-element.5) | copy-start | bytes 148

commit v4 on v0

v4 whole, which is shorter than its diff:
```python
import jax
import jax.numpy as jnp
from jax import lax
from jax.experimental import pallas as pl
from jax.experimental.pallas import tpu as pltpu
from jax.sharding import PartitionSpec as P

MESH = pl.DeviceIdType.MESH
BF, F32 = jnp.bfloat16, jnp.float32
BS = 64
ATOM_DEV = 4
N, OWN = 4096, 32
TALL, SLIM = 512, 256
ROWS, WIDE = 256, 512
CHUNKS = 4
CHUNK = ROWS // CHUNKS
PLANE, ROW = 16, 5


class Place:
    def __init__(self):
        row, col = lax.axis_index("row"), lax.axis_index("col")
        self.row, self.col = row, col
        self.zl = col // 8
        self.x, self.y, self.z, self.k = (col // 2) % 4, row // 2, (row % 2) * 2 + col // 8, col % 2
        self.own = self.x * 2 + self.k

    def at(self, x, y, z, k):
        return (y * 2 + z // 2, (z % 2) * 8 + x * 2 + k)

    def by(self, dx=0, dy=0, dz=0, dk=0):
        return self.at((self.x + dx) % 4, (self.y + dy) % 4, (self.z + dz) % 4, (self.k + dk) % 2)

    def partner(self):
        return (self.row, (self.col + 8) % 16)

    def line(self, dx, dk=0):
        return (self.x + dx) % 4 * 2 + (self.k + dk) % 2


class Copies:
    def __init__(self, me, send_sems, recv_sems):
        self.send_sems, self.recv_sems, self.any = send_sems, recv_sems, me.by(dx=1)

    def make(self, src, dst, send, recv, device):
        return pltpu.make_async_remote_copy(
            src_ref=src,
            dst_ref=dst,
            send_sem=self.send_sems.at[send],
            recv_sem=self.recv_sems.at[recv],
            device_id=device,
            device_id_type=MESH,
        )

    def send(self, src, dst, send, recv, device):
        self.make(src, dst, send, recv, device).start()

    def arrive(self, ref, recv):
        self.make(ref, ref, 0, recv, self.any).wait_recv()

    def sent(self, ref, send):
        self.make(ref, ref, send, 0, self.any).wait_send()


def chunk_piece(buf, first):
    def piece(y, z, t, lo, size):
        start = (y * 4 + z) * ROWS + (first + t) * CHUNK + lo
        return buf.at[pl.ds(pl.multiple_of(start, 32), size)]

    return piece


def tall_piece(buf, first, rows, swap=0):
    def piece(y, z, t, lo, size):
        start = (y * 2 + z // 2) * TALL + first + (t + swap * z) % 2 * rows + lo
        return buf.at[
            pl.ds(pl.multiple_of(start, 64), size), pl.ds(pl.multiple_of(z % 2 * SLIM, SLIM), SLIM)
        ]

    return piece


class Plane:
    def __init__(self, cp, me, buf, piece, rows, width, send, recv):
        self.cp, self.me, self.buf, self.piece = cp, me, buf, piece
        self.rows, self.send, self.recv = rows, send, recv
        self.equal = rows * width // WIDE

    def ref(self, t, i, j, lo=0, size=None):
        back = (i, j) if t == 0 else (j, i)
        y, z = (self.me.y + 4 - back[0]) % 4, (self.me.z + 4 - back[1]) % 4
        return self.piece(y, z, t, lo, self.rows if size is None else size)

    def put(self, t, i, j, axis, d, sem, lo=0, size=None):
        ref = self.ref(t, i, j, lo, size)
        device = self.me.by(dy=d) if axis == t else self.me.by(dz=d)
        self.cp.send(ref, ref, self.send, self.recv + sem, device)

    def got(self, sem, pieces=1):
        self.cp.arrive(self.buf.at[: pieces * self.equal], self.recv + sem)

    def start_first(self, t):
        self.put(t, 0, 0, 0, 1, 7 * t)
        self.put(t, 0, 0, 0, 3, 7 * t + 1)

    def start_second(self, t):
        self.put(t, 0, 0, 1, 1, 7 * t + 3)
        self.put(t, 0, 0, 1, 3, 7 * t + 3)

    def start(self, *ts):
        for t in ts:
            self.start_first(t)
        for t in ts:
            self.start_second(t)

    def first_ring(self, t):
        half = self.rows // 2
        self.got(7 * t)
        self.put(t, 1, 0, 0, 1, 7 * t + 2, 0, half)
        self.got(7 * t + 1)
        self.put(t, 3, 0, 0, 3, 7 * t + 2, half, half)
        self.put(t, 1, 0, 1, 1, 14)
        self.put(t, 1, 0, 1, 3, 7 * t + 4)
        self.put(t, 3, 0, 1, 1, 7 * t + 5)
        self.put(t, 3, 0, 1, 3, 14)

    def second_own(self, t):
        self.got(7 * t + 3, 2)
        self.put(t, 0, 1, 1, 1, 15)

    def first_far(self, t):
        self.got(7 * t + 2)
        self.put(t, 2, 0, 1, 1, 14)
        self.put(t, 2, 0, 1, 3, 7 * t + 6)

    def second_left(self, t):
        self.got(7 * t + 4)
        self.put(t, 1, 3, 1, 3, 15)

    def second_right(self, t):
        self.got(7 * t + 5)
        self.put(t, 3, 1, 1, 1, 15)

    def second_far(self, t):
        self.got(7 * t + 6)
        self.put(t, 2, 3, 1, 3, 15)

    def near(self):
        self.got(14, 6)

    def far(self):
        self.got(15, 8)

    def drain(self):
        self.cp.sent(self.buf.at[: 30 * self.equal], self.send)


class Row:
    def __init__(self, cp, me, buf, send, recv, lo=0, size=CHUNK):
        self.cp, self.me, self.buf, self.send, self.recv = cp, me, buf, send, recv
        self.lo, self.size = lo, size

    def put(self, d, to, sem, dk=0):
        at = pl.multiple_of(self.me.line(4 - d) * WIDE, WIDE)
        ref = self.buf.at[self.lo : self.lo + self.size, pl.ds(at, WIDE)]
        self.cp.send(ref, ref, self.send, self.recv + sem, self.me.by(dx=to, dk=dk))

    def got(self, sem, tiles=1):
        self.cp.arrive(self.buf.at[: self.size, : tiles * WIDE], self.recv + sem)

    def start(self):
        self.put(0, 1, 0)
        self.put(0, 3, 0)
        self.put(0, 2, 1)
        self.put(0, 0, 2, dk=1)

    def arrive(self):
        self.got(0, 2)
        self.put(1, 0, 3, dk=1)
        self.put(3, 0, 3, dk=1)
        self.got(1)
        self.put(2, 0, 4, dk=1)

    def shared_own(self):
        self.got(2)

    def shared(self):
        self.got(3, 2)
        self.got(4)


def dot(a, b):
    return jnp.dot(a, b, preferred_element_type=F32)


def block_k(b, zl):
    return pl.ds(pl.multiple_of((zl * 8 + b) * ROWS, ROWS), ROWS)


class Product:
    def __init__(self, left, right, lo=0, size=ROWS):
        self.left, self.right, self.rows, self.total = left, right, slice(lo, lo + size), None

    def add(self, b, zl):
        at = pl.ds(pl.multiple_of(b * WIDE + zl * SLIM, SLIM), SLIM)
        term = dot(self.left[self.rows, at], self.right[block_k(b, zl)])
        self.total = term if self.total is None else self.total + term

    def tiles(self, me, dk, *ds):
        for d in ds:
            for zl in range(2):
                self.add(me.line(4 - d, dk), zl)

    def blocks(self, me, pairs):
        for dy, dz in pairs:
            r = (me.y + 4 - dy) % 4 * 4 + (me.z + 4 - dz) % 4
            self.add(r % 8, r // 8)


EARLY = [(dy, dz) for dy in (0, 1, 3) for dz in (0, 1, 3)]
LATE = [(d, 2) for d in range(4)] + [(2, d) for d in (0, 1, 3)]


def mask_row(blocks, i):
    count = blocks.shape[0]
    lane = lax.broadcasted_iota(jnp.int32, (1, count * BS), 1) // BS
    row = jnp.zeros((1, count * BS), F32)
    for j in range(count):
        row = jnp.where(lane == j, blocks[j : j + 1, i : i + 1], row)
    return row


def kernel(
    hamil_hbm, guess_hbm, pattern_hbm, filters_hbm, deriv_hbm, atoms_hbm,
    energy_out, forces_out,
    hamil, guess, pattern, filters, deriv, atoms,
    rowp, colp, srow, grow, hcol, square, etile, eall, others, load_sems, send_sems, recv_sems,
):
    me = Place()
    cp = Copies(me, send_sems, recv_sems)
    peers = [me.by(dx=dx, dk=dk) for dx in range(4) for dk in range(2)][1:]
    peers += [me.by(dy=1), me.by(dy=3), me.by(dz=1), me.by(dz=3)]
    barrier = pltpu.get_barrier_semaphore()
    for peer in peers:
        pl.semaphore_signal(barrier, inc=1, device_id=peer, device_id_type=MESH)

    pairs = [(pattern_hbm, pattern), (guess_hbm, guess), (hamil_hbm, hamil)]
    pairs += [(filters_hbm, filters), (deriv_hbm, deriv), (atoms_hbm, atoms)]
    loads = [pltpu.make_async_copy(a, b, load_sems.at[i]) for i, (a, b) in enumerate(pairs)]
    for load in loads:
        load.start()
    for load in loads[:4]:
        load.wait()

    tall = pl.ds(pl.multiple_of(me.row * TALL, TALL), TALL)
    slim = pl.ds(pl.multiple_of(me.zl * SLIM, SLIM), SLIM)
    own_guess, own_ham = colp.at[0].at[tall, slim], hcol.at[tall, slim]
    kept = pattern[...].astype(F32)
    for i in range(TALL // BS):
        part = slice(i * BS, (i + 1) * BS)
        keep = mask_row(kept, i)
        here = me.row * TALL + i * BS + lax.broadcasted_iota(jnp.int32, (BS, SLIM), 0)
        there = me.col * SLIM + lax.broadcasted_iota(jnp.int32, (BS, SLIM), 1)
        half = jnp.where(here == there, 0.5, 0.0).astype(F32)
        own_guess[part] = ((half + guess[part].astype(F32)) * keep).astype(BF)
        own_ham[part] = jnp.where(keep > 0, hamil[part].astype(F32), 0.0).astype(BF)
    pl.semaphore_wait(barrier, len(peers))

    mine = pl.ds(pl.multiple_of((me.y * 4 + me.z) * ROWS, ROWS), ROWS)
    own_rows = pl.ds(pl.multiple_of(me.own * WIDE, WIDE), WIDE)
    chunk = [slice(c * CHUNK, (c + 1) * CHUNK) for c in range(CHUNKS)]
    row_sems = CHUNKS * ROW
    planes = 3 * row_sems
    plane_sems = [[planes], [planes + PLANE, planes + 2 * PLANE], [planes, planes + 3 * PLANE]]
    ham_sems = [planes + 4 * PLANE, planes + 5 * PLANE]
    filters_sem, energy_sem = planes + 6 * PLANE, planes + 6 * PLANE + 1

    def row_chunks(buf, send, group):
        return [Row(cp, me, buf, send, group * row_sems + c * ROW, c * CHUNK) for c in range(CHUNKS)]

    def drain_rows(buf, send):
        cp.sent(buf.at[:, : 7 * WIDE], send)

    cp.send(filters, others, 6, filters_sem, me.partner())
    panel = colp.at[0]
    plane = Plane(cp, me, panel, tall_piece(panel, 0, TALL // 2, 1), TALL // 2, SLIM, 2, plane_sems[0][0])
    rows = Row(cp, me, rowp, 0, 0, 0, ROWS)
    plane.start(0, 1)
    plane.first_ring(1)
    rowp[:, own_rows] = panel[mine]
    rows.start()
    plane.first_ring(0)
    for stage in (plane.second_own, plane.first_far, plane.second_left, plane.second_right, plane.second_far):
        stage(0)
        stage(1)
    rows.arrive()
    plane.near()
    rows.shared_own()
    rows.shared()
    first = Product(rowp, panel)
    first.blocks(me, EARLY)
    plane.far()
    plane.drain()
    cp.arrive(others, filters_sem)

    for step in range(2):
        drain_rows(rowp, 0)
        ham_piece = tall_piece(hcol, step * (TALL // 2), TALL // 4)
        ham = Plane(cp, me, hcol, ham_piece, TALL // 4, SLIM, 4 + step, ham_sems[step])
        inner = row_chunks(srow, 1, 1)
        thirds = []
        for c in range(CHUNKS):
            tail = Product(rowp, panel, c * CHUNK, CHUNK)
            tail.total = first.total[chunk[c]]
            tail.blocks(me, LATE)
            srow[chunk[c], own_rows] = tail.total.astype(BF)
            inner[c].start()
            if c == 0:
                ham.start(0, 1)
            square[chunk[c]] = tail.total
            thirds.append(Product(srow, panel, c * CHUNK, CHUNK))

        after = colp.at[(step + 1) % 2]
        own_piece, own_block = after.at[mine], rowp.at[:, own_rows]
        first_sem, second_sem = plane_sems[step + 1]
        pair = [
            Plane(cp, me, after, chunk_piece(after, 0), CHUNK, WIDE, 2 + (step + 1) % 2, first_sem),
            Plane(cp, me, after, chunk_piece(after, 2), CHUNK, WIDE, 2 + (step + 1) % 2, second_sem),
        ]
        rows = row_chunks(rowp, 0, 0)
        blocks = [filters[step].astype(F32), others[step].astype(F32)]
        keep = [jnp.where(me.zl == 0, m[:, :4], m[:, 4:]) for m in blocks]
        left = jnp.where(me.zl == 0, keep[0], keep[1])
        right = jnp.where(me.zl == 0, keep[1], keep[0])

        def finish(c):
            third = thirds[c]
            third.tiles(me, 0, 0)
            inner[c].shared_own()
            third.tiles(me, 1, 0)
            inner[c].arrive()
            third.tiles(me, 0, 1, 3, 2)
            inner[c].shared()
            third.tiles(me, 1, 1, 3, 2)
            mask = jnp.concatenate([mask_row(left, c), mask_row(right, c)], axis=1)
            dens = (mask * (3.0 * square[chunk[c]] - 2.0 * third.total)).astype(BF)
            own_piece[chunk[c]] = dens
            own_block[chunk[c]] = dens
            pair[c // 2].start(c % 2)
            if c == CHUNKS - 1:
                drain_rows(srow, 1)
            rows[c].start()

        def both(stage):
            stage(0)
            stage(1)

        both(ham.first_ring)
        both(ham.second_own)
        finish(0)
        both(ham.first_far)
        finish(1)
        both(ham.second_left)
        both(ham.second_right)
        pair[0].first_ring(0)
        pair[0].second_own(0)
        finish(2)
        both(ham.second_far)
        pair[0].first_ring(1)
        pair[0].second_own(1)
        finish(3)
        pair[0].first_far(0)
        pair[0].second_left(0)
        ham.near()
        ham.far()

        panel = after
        if step == 0:
            rows[0].arrive()
            pair[0].second_right(0)
            pair[1].first_ring(0)
            pair[1].second_own(0)
            pair[0].first_far(1)
            pair[0].second_left(1)
            rows[1].arrive()
            pair[0].second_far(0)
            pair[0].second_right(1)
            pair[1].first_ring(1)
            pair[1].second_own(1)
            pair[1].first_far(0)
            rows[2].arrive()
            pair[1].second_left(0)
            pair[0].second_far(1)
            pair[1].second_right(0)
            pair[1].first_far(1)
            pair[1].second_left(1)
            rows[3].arrive()
            pair[1].second_far(0)
            pair[1].second_right(1)
            pair[1].second_far(1)
            for row in rows:
                row.shared_own()
                row.shared()
            pair[0].near()
            pair[0].far()
            pair[1].near()
            first = Product(rowp, panel)
            first.blocks(me, EARLY)
            pair[1].far()
        else:
            energy_rows = row_chunks(grow, 7, 2)

            def inward(c):
                rows[c].shared_own()
                rows[c].shared()
                part = Product(rowp, hcol, c * CHUNK, CHUNK)
                part.tiles(me, 0, 0, 1, 3, 2)
                part.tiles(me, 1, 0, 1, 3, 2)
                grow[chunk[c], own_rows] = part.total.astype(BF)
                energy_rows[c].start()

            rows[0].arrive()
            pair[0].second_right(0)
            pair[1].first_ring(0)
            inward(0)
            pair[1].second_own(0)
            pair[0].first_far(1)
            pair[0].second_left(1)
            rows[1].arrive()
            pair[0].second_far(0)
            pair[0].second_right(1)
            pair[1].first_ring(1)
            inward(1)
            pair[1].second_own(1)
            pair[1].first_far(0)
            rows[2].arrive()
            pair[1].second_left(0)
            pair[0].second_far(1)
            pair[1].second_right(0)
            inward(2)
            pair[1].first_far(1)
            pair[1].second_left(1)
            rows[3].arrive()
            pair[1].second_far(0)
            energy_rows[0].arrive()
            inward(3)
            pair[1].second_right(1)
            pair[1].second_far(1)
            energy_rows[1].arrive()
            pair[0].near()
            pair[0].far()
            pair[1].near()
            energy_rows[2].arrive()
            for c in range(3):
                energy_rows[c].shared_own()
                energy_rows[c].shared()
            pair[1].far()
            upper, lower = Product(grow, panel, 0, 3 * CHUNK), Product(grow, panel, 3 * CHUNK, CHUNK)
            for dk in range(2):
                upper.tiles(me, dk, 0, 1, 3, 2)
            etile[: 3 * CHUNK] = upper.total.astype(BF)
            lower.tiles(me, 0, 0)
            energy_rows[3].shared_own()
            lower.tiles(me, 1, 0)
            energy_rows[3].arrive()
            lower.tiles(me, 0, 1, 3, 2)
            energy_rows[3].shared()
            lower.tiles(me, 1, 1, 3, 2)
            etile[3 * CHUNK :] = lower.total.astype(BF)
            drain_rows(rowp, 0)
            drain_rows(grow, 7)
        both_sent = after.at[: 60 * CHUNK]
        cp.sent(both_sent, 2 + (step + 1) % 2)
        ham.drain()

    rels = [(dx, dk) for dx in (2, 1, 3, 0) for dk in range(2)][:-2] + [(0, 1)]
    for dx, dk in rels:
        src = etile.at[pl.ds(pl.multiple_of(me.line(dx, dk) * OWN, OWN), OWN)]
        cp.send(src, eall.at[:, own_rows], 0, energy_sem, me.by(dx=dx, dk=dk))
    eall[:, own_rows] = etile[pl.ds(pl.multiple_of(me.own * OWN, OWN), OWN)]
    same = lax.broadcasted_iota(jnp.int32, (OWN, OWN), 0) == lax.broadcasted_iota(jnp.int32, (OWN, OWN), 1)
    loads[4].wait()
    loads[5].wait()
    atom_of = jnp.sum(jnp.where(same, atoms[...].astype(F32), 0.0), axis=1, keepdims=True)
    cp.sent(filters, 6)
    cp.arrive(eall.at[:, : 7 * WIDE], energy_sem)
    for b in range(8):
        for zl in range(2):
            energy_out[:, (zl * 8 + b) * SLIM : (zl * 8 + b + 1) * SLIM] = eall[
                :, b * WIDE + zl * SLIM : b * WIDE + (zl + 1) * SLIM
            ]
    wide = energy_out[...].astype(F32)
    line = lax.broadcasted_iota(jnp.int32, (3, ATOM_DEV), 0)
    lane = lax.broadcasted_iota(jnp.int32, (3, ATOM_DEV), 1)
    forces = jnp.zeros((3, ATOM_DEV), F32)
    for axis in range(3):
        per_row = jnp.sum(deriv[axis].astype(F32) * wide, axis=1, keepdims=True)
        for atom in range(ATOM_DEV):
            force = jnp.sum(jnp.where(atom_of == atom, per_row, 0.0))
            forces = jnp.where((line == axis) & (lane == atom), force, forces)
    forces_out[...] = forces
    cp.sent(eall.at[:, : 7 * WIDE], 0)


def body(hamil, guess, pattern, filters, deriv, atom_of_row):
    args = (hamil, guess, pattern.T, filters.transpose(0, 2, 1), deriv, atom_of_row.reshape(1, OWN))
    vmem = pl.BlockSpec(memory_space=pltpu.VMEM)
    return pl.pallas_call(
        kernel,
        out_shape=(
            jax.ShapeDtypeStruct((OWN, N), BF),
            jax.ShapeDtypeStruct((3, ATOM_DEV), F32),
        ),
        in_specs=[pl.BlockSpec(memory_space=pl.ANY)] * 6,
        out_specs=(vmem, vmem),
        scratch_shapes=[pltpu.VMEM(arg.shape, arg.dtype) for arg in args]
        + [
            pltpu.VMEM((ROWS, N), BF),
            pltpu.VMEM((2, N, WIDE), BF),
            pltpu.VMEM((ROWS, N), BF),
            pltpu.VMEM((ROWS, N), BF),
            pltpu.VMEM((N, WIDE), BF),
            pltpu.VMEM((ROWS, WIDE), F32),
            pltpu.VMEM((ROWS, WIDE), BF),
            pltpu.VMEM((OWN, N), BF),
            pltpu.VMEM(args[3].shape, args[3].dtype),
            pltpu.SemaphoreType.DMA((6,)),
            pltpu.SemaphoreType.DMA((8,)),
            pltpu.SemaphoreType.DMA((3 * CHUNKS * ROW + 6 * PLANE + 2,)),
        ],
        compiler_params=pltpu.CompilerParams(
            collective_id=0, has_side_effects=True, vmem_limit_bytes=60 * 1024 * 1024
        ),
    )(*args)


def solution(mesh):
    return jax.shard_map(
        body,
        mesh=mesh,
        in_specs=(
            P("row", "col"),
            P("row", "col"),
            P("row", "col"),
            P(None, "row", "col"),
            P(None, ("row", "col"), None),
            P(("row", "col")),
        ),
        out_specs=(P(("row", "col"), None), P(None, ("row", "col"))),
        check_vma=False,
    )
```

time: 544 us -> 126 us (0.23)
  waiting for transfers between devices: 482 us -> 0 us
  Pallas kernels: 0 us -> 123 us
  matrix products: 30.7 us -> 0 us
  between operations: 14.3 us -> 0.65 us
  blocking collectives: 11.5 us -> 0 us
    all_gather x10 -> x0, waiting for transfers between devices: 480 us -> none  [the longest x6 257 us: fold_rows(): lax.all_gather(left_tile, 'col', axis=1, tiled=True)]
    pallas_call x0 -> x1, Pallas kernels: none -> 123 us  [body(): pl.pallas_call(kernel, out_shape=(jax.ShapeDtypeStruct((OWN, N), BF), jax...]
    dot_general x8 -> x0, matrix products: 30.7 us -> none  [the longest x6 28.4 us: fold_rows(): jnp.dot(lax.all_gather(left_tile, 'col', axis=1, tiled=True), right_panel...]
    all_to_all x1 -> x0, blocking collectives: 11.5 us -> none  [body(): lax.all_to_all(energy, 'col', split_axis=0, concat_axis=1, tiled=True)]
  transfers between devices with their start and end apart: 10 -> 0, of which waited for: 10 -> 0; matrix products, arithmetic and copies ran while one was open for 1% -> 0% of each run, Pallas kernels for 0% -> 0%
where the time goes in v4:
time: 126 us
  Pallas kernels  123 us (98%)
  local copies, waits for them, and re-layouts  2.25 us (2%)
    pallas_call x1, Pallas kernels, body(): pl.pallas_call(kernel, out_shape=(jax.ShapeDtypeStruct((OWN, N), BF), jax...  123 us

profile of v4, /device:TPU:1, one launch (start us, length us, event | category | flops | bytes accessed | tf_op | source)
XLA Modules:
  0.0 125.6 jit_solution(16920301641665418087)
XLA Ops:
  0.6 122.7 %shard_map.77 = (bf16[32,4096]{1,0:T(8,128)(2,1)}, f32[3,4]{1,0:T(4,128)}) custom-call(bf16[512,256]{1,0:T(8,128)(2,1)} %hamil_hbm.1, bf16[512,256]{1,0:T(8,128)(2,1)} %guess_hbm.1, s32[4,8]{1,0:T(4,128)} %bitcast.4, s32[2,4,8]{2,1,0:T(4,128)} %bitcast.3, bf16[3,32,4096]{2,1,0:T(8,128)(2,1)} %deriv_hbm.1, s32[1,32]{1,0:T(1,128)} %bitcast.5), custom_call_target="tpu_custom_call" | custom-call | tf_op jit(solution)/shard_map/pallas_call | solution.py:508
  123.3 0.0 copy-start
  123.3 1.7 %copy.10 = bf16[32,4096]{1,0:T(8,128)(2,1)} copy(bf16[32,4096]{1,0:T(8,128)(2,1)} %get-tuple-element.4) | data formatting | bytes 524288
  125.0 0.0 copy-done
  125.0 0.6 copy.11
Async XLA Ops:
  123.3 1.7 %copy-start = (f32[3,4]{1,0:T(4,128)S(1)}, f32[3,4]{1,0:T(4,128)}, u32[]{:S(2)}) copy-start(f32[3,4]{1,0:T(4,128)} %get-tuple-element.5) | copy-start | bytes 148

commit v5 on v4

--- a/solution.py
+++ b/solution.py
@@ -1,3 +1,5 @@
+import functools
+
 import jax
 import jax.numpy as jnp
 from jax import lax
@@ -99,51 +101,53 @@
     def got(self, sem, pieces=1):
         self.cp.arrive(self.buf.at[: pieces * self.equal], self.recv + sem)
 
-    def start_first(self, t):
+    def own_first(self, t):
         self.put(t, 0, 0, 0, 1, 7 * t)
         self.put(t, 0, 0, 0, 3, 7 * t + 1)
 
-    def start_second(self, t):
+    def own_second(self, t):
         self.put(t, 0, 0, 1, 1, 7 * t + 3)
         self.put(t, 0, 0, 1, 3, 7 * t + 3)
 
-    def start(self, *ts):
-        for t in ts:
-            self.start_first(t)
-        for t in ts:
-            self.start_second(t)
-
-    def first_ring(self, t):
+    def ring(self, t):
         half = self.rows // 2
         self.got(7 * t)
         self.put(t, 1, 0, 0, 1, 7 * t + 2, 0, half)
         self.got(7 * t + 1)
         self.put(t, 3, 0, 0, 3, 7 * t + 2, half, half)
-        self.put(t, 1, 0, 1, 1, 14)
+
+    def spread(self, t):
         self.put(t, 1, 0, 1, 3, 7 * t + 4)
         self.put(t, 3, 0, 1, 1, 7 * t + 5)
+        self.put(t, 1, 0, 1, 1, 14)
         self.put(t, 3, 0, 1, 3, 14)
 
-    def second_own(self, t):
+    def own_far(self, t):
         self.got(7 * t + 3, 2)
         self.put(t, 0, 1, 1, 1, 15)
 
-    def first_far(self, t):
+    def spread_far(self, t):
         self.got(7 * t + 2)
+        self.put(t, 2, 0, 1, 3, 7 * t + 6)
         self.put(t, 2, 0, 1, 1, 14)
-        self.put(t, 2, 0, 1, 3, 7 * t + 6)
-
-    def second_left(self, t):
+
+    def left_far(self, t):
         self.got(7 * t + 4)
         self.put(t, 1, 3, 1, 3, 15)
 
-    def second_right(self, t):
+    def right_far(self, t):
         self.got(7 * t + 5)
         self.put(t, 3, 1, 1, 1, 15)
 
-    def second_far(self, t):
+    def far_far(self, t):
         self.got(7 * t + 6)
         self.put(t, 2, 3, 1, 3, 15)
+
+    def tasks(self, name):
+        steps = [self.own_first, self.own_second, self.ring, self.spread, self.own_far]
+        steps += [self.spread_far, self.left_far, self.right_far, self.far_far]
+        out = {name + str(t) + l: functools.partial(f, t) for l, f in zip("abcdefghi", steps) for t in range(2)}
+        return {**out, name + "n": self.near, name + "z": self.far}
 
     def near(self):
         self.got(14, 6)
@@ -228,6 +232,33 @@
     for j in range(count):
         row = jnp.where(lane == j, blocks[j : j + 1, i : i + 1], row)
     return row
+
+
+def run(tasks, order):
+    for name in order:
+        tasks[name]()
+
+
+ORDER_A = [
+    "A0a", "A1a", "A1b", "A0b", "A0c", "A1c", "A1d", "A0d", "R", "A0e", "A0f", "A1f", "A1g", "A1e", "A0h", "A0g",
+    "A1h", "A1i", "A0i", "Ra", "Rs", "An", "E", "Az",
+]
+ORDER_B = [
+    "H1a", "H0a", "S0", "S1", "S2", "H1b", "H0b", "H1c", "H0c", "H0d", "S3", "H1d", "T0", "H0e", "H1f", "H0f", "D0",
+    "P0b", "H1e", "P0a", "H1g", "H0g", "T1", "D1", "P1a", "R1", "P1b", "T2", "H1h", "H1i", "H0i", "H0h", "D2",
+    "Q0b", "Q0a", "T3", "P0c", "P1c", "P1d", "D3", "Q1a", "P0d", "Hz", "R0", "R3", "Q1b", "P0f", "R2", "Q0c", "Q1c",
+    "P1f", "Q0d", "P1g", "Q1d", "Q0f", "P0i", "P0g", "P0e", "Q1e", "Q0e", "P0h", "P1e", "Ra3", "Q1f", "P1i", "Q0h",
+    "P1h", "Ra2", "Rs3", "Q1g", "Ra0", "Q0g", "Ra1", "Pn", "Q0i", "Q1i", "Q1h", "Qn", "Rs1", "Pz", "Rs0", "Rs2",
+    "E", "Hn", "Qz",
+]
+ORDER_C = [
+    "S0", "H1a", "H0a", "S1", "S2", "H0b", "S3", "H1b", "H1c", "H0c", "H0d", "H1d", "T0", "H0e", "H1f", "H0f", "D0",
+    "T1", "H0g", "R0", "P0a", "H1g", "P0b", "D1", "P1b", "P1a", "H1h", "H0h", "T2", "R1", "H0i", "D2", "Q0a", "H1i",
+    "Q0b", "T3", "H1e", "P0c", "R2", "D3", "Q1a", "P1c", "Q1b", "R3", "Q0c", "Ra0", "Hn", "P1d", "Q0d", "Rs0", "Hz",
+    "G0", "Q1c", "P0f", "Ra1", "P0e", "Q1d", "Ra2", "Rs1", "P1f", "P0d", "G1", "Q1f", "P1g", "Q0h", "Q1e", "Q0e",
+    "Rs2", "Q0f", "P1e", "P0i", "G2", "Q0g", "Ra3", "P1h", "Q1g", "Rs3", "P0g", "Q1h", "P1i", "P0h", "Q1i", "Q0i",
+    "G3", "La0", "La1", "Ls0", "La2", "Ls1", "Pn", "Qn", "Ls2", "Pz", "Qz", "U", "La3", "Ls3", "V",
+]
 
 
 def kernel(
@@ -284,199 +315,125 @@
     cp.send(filters, others, 6, filters_sem, me.partner())
     panel = colp.at[0]
     plane = Plane(cp, me, panel, tall_piece(panel, 0, TALL // 2, 1), TALL // 2, SLIM, 2, plane_sems[0][0])
-    rows = Row(cp, me, rowp, 0, 0, 0, ROWS)
-    plane.start(0, 1)
-    plane.first_ring(1)
-    rowp[:, own_rows] = panel[mine]
-    rows.start()
-    plane.first_ring(0)
-    for stage in (plane.second_own, plane.first_far, plane.second_left, plane.second_right, plane.second_far):
-        stage(0)
-        stage(1)
-    rows.arrive()
-    plane.near()
-    rows.shared_own()
-    rows.shared()
+    whole = Row(cp, me, rowp, 0, 0, 0, ROWS)
     first = Product(rowp, panel)
-    first.blocks(me, EARLY)
-    plane.far()
+
+    def whole_start():
+        rowp[:, own_rows] = colp[0, mine]
+        whole.start()
+
+    def whole_shared():
+        whole.shared_own()
+        whole.shared()
+
+    tasks = plane.tasks("A")
+    tasks.update(R=whole_start, Ra=whole.arrive, Rs=whole_shared, E=lambda: first.blocks(me, EARLY))
+    run(tasks, ORDER_A)
     plane.drain()
     cp.arrive(others, filters_sem)
 
     for step in range(2):
         drain_rows(rowp, 0)
+        panel, after = colp.at[step], colp.at[1 - step]
         ham_piece = tall_piece(hcol, step * (TALL // 2), TALL // 4)
         ham = Plane(cp, me, hcol, ham_piece, TALL // 4, SLIM, 4 + step, ham_sems[step])
-        inner = row_chunks(srow, 1, 1)
-        thirds = []
-        for c in range(CHUNKS):
-            tail = Product(rowp, panel, c * CHUNK, CHUNK)
-            tail.total = first.total[chunk[c]]
-            tail.blocks(me, LATE)
-            srow[chunk[c], own_rows] = tail.total.astype(BF)
-            inner[c].start()
-            if c == 0:
-                ham.start(0, 1)
-            square[chunk[c]] = tail.total
-            thirds.append(Product(srow, panel, c * CHUNK, CHUNK))
-
-        after = colp.at[(step + 1) % 2]
+        pair = [
+            Plane(cp, me, after, chunk_piece(after, 2 * i), CHUNK, WIDE, 3 - step, plane_sems[step + 1][i])
+            for i in range(2)
+        ]
+        inner, rows, last = row_chunks(srow, 1, 1), row_chunks(rowp, 0, 0), row_chunks(grow, 7, 2)
+        thirds = [Product(srow, panel, c * CHUNK, CHUNK) for c in range(CHUNKS)]
         own_piece, own_block = after.at[mine], rowp.at[:, own_rows]
-        first_sem, second_sem = plane_sems[step + 1]
-        pair = [
-            Plane(cp, me, after, chunk_piece(after, 0), CHUNK, WIDE, 2 + (step + 1) % 2, first_sem),
-            Plane(cp, me, after, chunk_piece(after, 2), CHUNK, WIDE, 2 + (step + 1) % 2, second_sem),
-        ]
-        rows = row_chunks(rowp, 0, 0)
         blocks = [filters[step].astype(F32), others[step].astype(F32)]
         keep = [jnp.where(me.zl == 0, m[:, :4], m[:, 4:]) for m in blocks]
         left = jnp.where(me.zl == 0, keep[0], keep[1])
         right = jnp.where(me.zl == 0, keep[1], keep[0])
-
-        def finish(c):
-            third = thirds[c]
-            third.tiles(me, 0, 0)
+        early = first.total
+        upper, lower = Product(grow, after, 0, 3 * CHUNK), Product(grow, after, 3 * CHUNK, CHUNK)
+
+        def square_chunk(c):
+            tail = Product(rowp, panel, c * CHUNK, CHUNK)
+            tail.total = early[chunk[c]]
+            tail.blocks(me, LATE)
+            srow[chunk[c], own_rows] = tail.total.astype(BF)
+            inner[c].start()
+            square[chunk[c]] = tail.total
+
+        def third_chunk(c):
+            inner[c].arrive()
+            thirds[c].tiles(me, 0, 0, 1, 3, 2)
+
+        def dens_chunk(c):
             inner[c].shared_own()
-            third.tiles(me, 1, 0)
-            inner[c].arrive()
-            third.tiles(me, 0, 1, 3, 2)
             inner[c].shared()
-            third.tiles(me, 1, 1, 3, 2)
+            thirds[c].tiles(me, 1, 0, 1, 3, 2)
             mask = jnp.concatenate([mask_row(left, c), mask_row(right, c)], axis=1)
-            dens = (mask * (3.0 * square[chunk[c]] - 2.0 * third.total)).astype(BF)
+            dens = (mask * (3.0 * square[chunk[c]] - 2.0 * thirds[c].total)).astype(BF)
             own_piece[chunk[c]] = dens
             own_block[chunk[c]] = dens
-            pair[c // 2].start(c % 2)
+
+        def rows_start(c):
             if c == CHUNKS - 1:
                 drain_rows(srow, 1)
             rows[c].start()
 
-        def both(stage):
-            stage(0)
-            stage(1)
-
-        both(ham.first_ring)
-        both(ham.second_own)
-        finish(0)
-        both(ham.first_far)
-        finish(1)
-        both(ham.second_left)
-        both(ham.second_right)
-        pair[0].first_ring(0)
-        pair[0].second_own(0)
-        finish(2)
-        both(ham.second_far)
-        pair[0].first_ring(1)
-        pair[0].second_own(1)
-        finish(3)
-        pair[0].first_far(0)
-        pair[0].second_left(0)
-        ham.near()
-        ham.far()
-
-        panel = after
-        if step == 0:
-            rows[0].arrive()
-            pair[0].second_right(0)
-            pair[1].first_ring(0)
-            pair[1].second_own(0)
-            pair[0].first_far(1)
-            pair[0].second_left(1)
-            rows[1].arrive()
-            pair[0].second_far(0)
-            pair[0].second_right(1)
-            pair[1].first_ring(1)
-            pair[1].second_own(1)
-            pair[1].first_far(0)
-            rows[2].arrive()
-            pair[1].second_left(0)
-            pair[0].second_far(1)
-            pair[1].second_right(0)
-            pair[1].first_far(1)
-            pair[1].second_left(1)
-            rows[3].arrive()
-            pair[1].second_far(0)
-            pair[1].second_right(1)
-            pair[1].second_far(1)
-            for row in rows:
-                row.shared_own()
-                row.shared()
-            pair[0].near()
-            pair[0].far()
-            pair[1].near()
-            first = Product(rowp, panel)
-            first.blocks(me, EARLY)
-            pair[1].far()
-        else:
-            energy_rows = row_chunks(grow, 7, 2)
-
-            def inward(c):
-                rows[c].shared_own()
-                rows[c].shared()
-                part = Product(rowp, hcol, c * CHUNK, CHUNK)
-                part.tiles(me, 0, 0, 1, 3, 2)
-                part.tiles(me, 1, 0, 1, 3, 2)
-                grow[chunk[c], own_rows] = part.total.astype(BF)
-                energy_rows[c].start()
-
-            rows[0].arrive()
-            pair[0].second_right(0)
-            pair[1].first_ring(0)
-            inward(0)
-            pair[1].second_own(0)
-            pair[0].first_far(1)
-            pair[0].second_left(1)
-            rows[1].arrive()
-            pair[0].second_far(0)
-            pair[0].second_right(1)
-            pair[1].first_ring(1)
-            inward(1)
-            pair[1].second_own(1)
-            pair[1].first_far(0)
-            rows[2].arrive()
-            pair[1].second_left(0)
-            pair[0].second_far(1)
-            pair[1].second_right(0)
-            inward(2)
-            pair[1].first_far(1)
-            pair[1].second_left(1)
-            rows[3].arrive()
-            pair[1].second_far(0)
-            energy_rows[0].arrive()
-            inward(3)
-            pair[1].second_right(1)
-            pair[1].second_far(1)
-            energy_rows[1].arrive()
-            pair[0].near()
-            pair[0].far()
-            pair[1].near()
-            energy_rows[2].arrive()
-            for c in range(3):
-                energy_rows[c].shared_own()
-                energy_rows[c].shared()
-            pair[1].far()
-            upper, lower = Product(grow, panel, 0, 3 * CHUNK), Product(grow, panel, 3 * CHUNK, CHUNK)
+        def rows_shared(c):
+            rows[c].shared_own()
+            rows[c].shared()
+
+        def inward(c):
+            part = Product(rowp, hcol, c * CHUNK, CHUNK)
+            part.tiles(me, 0, 0, 1, 3, 2)
+            part.tiles(me, 1, 0, 1, 3, 2)
+            grow[chunk[c], own_rows] = part.total.astype(BF)
+            last[c].start()
+
+        def last_shared(c):
+            last[c].shared_own()
+            last[c].shared()
+
+        def give(c):
+            for dk in range(2):
+                k = (me.k + dk) % 2
+                src = etile.at[pl.ds(pl.multiple_of(c * CHUNK + k * OWN, OWN), OWN)]
+                target = me.by(dx=4 - me.x + c, dk=dk)
+
+                def send():
+                    cp.send(src, eall.at[:, own_rows], 8, energy_sem, target)
+
+                if dk:
+                    send()
+                else:
+                    pl.when(me.x != c)(send)
+
+        def energy_upper():
             for dk in range(2):
                 upper.tiles(me, dk, 0, 1, 3, 2)
             etile[: 3 * CHUNK] = upper.total.astype(BF)
-            lower.tiles(me, 0, 0)
-            energy_rows[3].shared_own()
-            lower.tiles(me, 1, 0)
-            energy_rows[3].arrive()
-            lower.tiles(me, 0, 1, 3, 2)
-            energy_rows[3].shared()
-            lower.tiles(me, 1, 1, 3, 2)
+            for c in range(3):
+                give(c)
+
+        def energy_lower():
+            for dk in range(2):
+                lower.tiles(me, dk, 0, 1, 3, 2)
             etile[3 * CHUNK :] = lower.total.astype(BF)
-            drain_rows(rowp, 0)
-            drain_rows(grow, 7)
-        both_sent = after.at[: 60 * CHUNK]
-        cp.sent(both_sent, 2 + (step + 1) % 2)
+            give(3)
+
+        tasks = {**ham.tasks("H"), **pair[0].tasks("P"), **pair[1].tasks("Q")}
+        steps = dict(S=square_chunk, T=third_chunk, D=dens_chunk, R=rows_start, Rs=rows_shared, G=inward, Ls=last_shared)
+        for c in range(CHUNKS):
+            tasks.update({name + str(c): functools.partial(f, c) for name, f in steps.items()})
+            tasks.update({"Ra" + str(c): rows[c].arrive, "La" + str(c): last[c].arrive})
+        if step == 0:
+            first = Product(rowp, after)
+            tasks.update(E=functools.partial(first.blocks, me, EARLY))
+        tasks.update(U=energy_upper, V=energy_lower)
+        run(tasks, ORDER_B if step == 0 else ORDER_C)
+        cp.sent(after.at[: 60 * CHUNK], 3 - step)
         ham.drain()
 
-    rels = [(dx, dk) for dx in (2, 1, 3, 0) for dk in range(2)][:-2] + [(0, 1)]
-    for dx, dk in rels:
-        src = etile.at[pl.ds(pl.multiple_of(me.line(dx, dk) * OWN, OWN), OWN)]
-        cp.send(src, eall.at[:, own_rows], 0, energy_sem, me.by(dx=dx, dk=dk))
+    drain_rows(rowp, 0)
+    drain_rows(grow, 7)
     eall[:, own_rows] = etile[pl.ds(pl.multiple_of(me.own * OWN, OWN), OWN)]
     same = lax.broadcasted_iota(jnp.int32, (OWN, OWN), 0) == lax.broadcasted_iota(jnp.int32, (OWN, OWN), 1)
     loads[4].wait()
@@ -499,7 +456,7 @@
             force = jnp.sum(jnp.where(atom_of == atom, per_row, 0.0))
             forces = jnp.where((line == axis) & (lane == atom), force, forces)
     forces_out[...] = forces
-    cp.sent(eall.at[:, : 7 * WIDE], 0)
+    cp.sent(eall.at[:, : 7 * WIDE], 8)
 
 
 def body(hamil, guess, pattern, filters, deriv, atom_of_row):
@@ -525,7 +482,7 @@
             pltpu.VMEM((OWN, N), BF),
             pltpu.VMEM(args[3].shape, args[3].dtype),
             pltpu.SemaphoreType.DMA((6,)),
-            pltpu.SemaphoreType.DMA((8,)),
+            pltpu.SemaphoreType.DMA((9,)),
             pltpu.SemaphoreType.DMA((3 * CHUNKS * ROW + 6 * PLANE + 2,)),
         ],
         compiler_params=pltpu.CompilerParams(

time: 126 us -> 115 us (0.913)
  Pallas kernels: 123 us -> 112 us
    pallas_call x1, Pallas kernels: 123 us -> 112 us  [body(): pl.pallas_call(kernel, out_shape=(jax.ShapeDtypeStruct((OWN, N), BF), jax...]
where the time goes in v5:
time: 115 us
  Pallas kernels  112 us (97%)
  local copies, waits for them, and re-layouts  2.25 us (2%)
    pallas_call x1, Pallas kernels, body(): pl.pallas_call(kernel, out_shape=(jax.ShapeDtypeStruct((OWN, N), BF), jax...  112 us

profile of v5, /device:TPU:1, one launch (start us, length us, event | category | flops | bytes accessed | tf_op | source)
XLA Modules:
  0.0 114.6 jit_solution(7384278404087051573)
XLA Ops:
  0.6 111.7 %shard_map.77 = (bf16[32,4096]{1,0:T(8,128)(2,1)}, f32[3,4]{1,0:T(4,128)}) custom-call(bf16[512,256]{1,0:T(8,128)(2,1)} %hamil_hbm.1, bf16[512,256]{1,0:T(8,128)(2,1)} %guess_hbm.1, s32[4,8]{1,0:T(4,128)} %bitcast.4, s32[2,4,8]{2,1,0:T(4,128)} %bitcast.3, bf16[3,32,4096]{2,1,0:T(8,128)(2,1)} %deriv_hbm.1, s32[1,32]{1,0:T(1,128)} %bitcast.5), custom_call_target="tpu_custom_call" | custom-call | tf_op jit(solution)/shard_map/pallas_call | solution.py:465
  112.4 0.0 copy-start
  112.4 1.7 %copy.10 = bf16[32,4096]{1,0:T(8,128)(2,1)} copy(bf16[32,4096]{1,0:T(8,128)(2,1)} %get-tuple-element.4) | data formatting | bytes 524288
  114.0 0.0 copy-done
  114.0 0.6 copy.11
Async XLA Ops:
  112.4 1.7 %copy-start = (f32[3,4]{1,0:T(4,128)S(1)}, f32[3,4]{1,0:T(4,128)}, u32[]{:S(2)}) copy-start(f32[3,4]{1,0:T(4,128)} %get-tuple-element.5) | copy-start | bytes 148

commit v6 on v5

--- a/solution.py
+++ b/solution.py
@@ -14,9 +14,8 @@
 N, OWN = 4096, 32
 TALL, SLIM = 512, 256
 ROWS, WIDE = 256, 512
-CHUNKS = 4
-CHUNK = ROWS // CHUNKS
-PLANE, ROW = 16, 5
+SIZES = [[64, 64, 64, 64], [64, 64, 64, 64]]
+PLANE, ROW = 16, 3
 
 
 class Place:
@@ -64,10 +63,10 @@
         self.make(ref, ref, send, 0, self.any).wait_send()
 
 
-def chunk_piece(buf, first):
+def chunk_piece(buf, first, rows):
     def piece(y, z, t, lo, size):
-        start = (y * 4 + z) * ROWS + (first + t) * CHUNK + lo
-        return buf.at[pl.ds(pl.multiple_of(start, 32), size)]
+        start = (y * 4 + z) * ROWS + first + t * rows + lo
+        return buf.at[pl.ds(pl.multiple_of(start, 16), size)]
 
     return piece
 
@@ -160,7 +159,7 @@
 
 
 class Row:
-    def __init__(self, cp, me, buf, send, recv, lo=0, size=CHUNK):
+    def __init__(self, cp, me, buf, send, recv, lo, size):
         self.cp, self.me, self.buf, self.send, self.recv = cp, me, buf, send, recv
         self.lo, self.size = lo, size
 
@@ -180,17 +179,13 @@
 
     def arrive(self):
         self.got(0, 2)
-        self.put(1, 0, 3, dk=1)
-        self.put(3, 0, 3, dk=1)
+        self.put(1, 0, 2, dk=1)
+        self.put(3, 0, 2, dk=1)
         self.got(1)
-        self.put(2, 0, 4, dk=1)
-
-    def shared_own(self):
-        self.got(2)
+        self.put(2, 0, 2, dk=1)
 
     def shared(self):
-        self.got(3, 2)
-        self.got(4)
+        self.got(2, 4)
 
 
 def dot(a, b):
@@ -240,24 +235,24 @@
 
 
 ORDER_A = [
-    "A0a", "A1a", "A1b", "A0b", "A0c", "A1c", "A1d", "A0d", "R", "A0e", "A0f", "A1f", "A1g", "A1e", "A0h", "A0g",
-    "A1h", "A1i", "A0i", "Ra", "Rs", "An", "E", "Az",
+    "A0a", "A1a", "A0b", "A1b", "A0c", "A1c", "R", "A1d", "A0d", "A1f", "A0f", "A1h", "A1g", "A0h", "A0g", "A1e",
+    "A1i", "A0e", "A0i", "H1a", "H0a", "H1b", "Ra", "Rs", "An", "H0b", "E", "Az",
 ]
 ORDER_B = [
-    "H1a", "H0a", "S0", "S1", "S2", "H1b", "H0b", "H1c", "H0c", "H0d", "S3", "H1d", "T0", "H0e", "H1f", "H0f", "D0",
-    "P0b", "H1e", "P0a", "H1g", "H0g", "T1", "D1", "P1a", "R1", "P1b", "T2", "H1h", "H1i", "H0i", "H0h", "D2",
-    "Q0b", "Q0a", "T3", "P0c", "P1c", "P1d", "D3", "Q1a", "P0d", "Hz", "R0", "R3", "Q1b", "P0f", "R2", "Q0c", "Q1c",
-    "P1f", "Q0d", "P1g", "Q1d", "Q0f", "P0i", "P0g", "P0e", "Q1e", "Q0e", "P0h", "P1e", "Ra3", "Q1f", "P1i", "Q0h",
-    "P1h", "Ra2", "Rs3", "Q1g", "Ra0", "Q0g", "Ra1", "Pn", "Q0i", "Q1i", "Q1h", "Qn", "Rs1", "Pz", "Rs0", "Rs2",
-    "E", "Hn", "Qz",
+    "S0", "S1", "H1c", "H0c", "H1d", "H0d", "S2", "S3", "H0e", "H1e", "H0f", "H1f", "H1g", "T0", "H0h", "H0g", "D0",
+    "P0b", "P0a", "H1h", "T1", "H0i", "H1i", "D1", "P1a", "P1b", "T2", "P0c", "R0", "P0d", "R1", "D2", "Q0a", "T3",
+    "P1c", "P1d", "D3", "Q1a", "R3", "Q0c", "Q0d", "Hn", "Q1b", "P1f", "Q1c", "P0f", "P1e", "Ra0", "Q1d", "Q0b",
+    "Q0f", "P0e", "Q1e", "P1g", "R2", "Q1f", "Q0h", "P1i", "P0g", "P1h", "P0h", "P0i", "Q1h", "Q1g", "Q0g", "Ra3",
+    "Rs3", "Q0i", "Hz", "Ra1", "Q0e", "Q1i", "Ra2", "Pn", "I0a", "Rs0", "Qn", "I1a", "Rs2", "Rs1", "Pz", "E", "I0b",
+    "Qz",
 ]
 ORDER_C = [
-    "S0", "H1a", "H0a", "S1", "S2", "H0b", "S3", "H1b", "H1c", "H0c", "H0d", "H1d", "T0", "H0e", "H1f", "H0f", "D0",
-    "T1", "H0g", "R0", "P0a", "H1g", "P0b", "D1", "P1b", "P1a", "H1h", "H0h", "T2", "R1", "H0i", "D2", "Q0a", "H1i",
-    "Q0b", "T3", "H1e", "P0c", "R2", "D3", "Q1a", "P1c", "Q1b", "R3", "Q0c", "Ra0", "Hn", "P1d", "Q0d", "Rs0", "Hz",
-    "G0", "Q1c", "P0f", "Ra1", "P0e", "Q1d", "Ra2", "Rs1", "P1f", "P0d", "G1", "Q1f", "P1g", "Q0h", "Q1e", "Q0e",
-    "Rs2", "Q0f", "P1e", "P0i", "G2", "Q0g", "Ra3", "P1h", "Q1g", "Rs3", "P0g", "Q1h", "P1i", "P0h", "Q1i", "Q0i",
-    "G3", "La0", "La1", "Ls0", "La2", "Ls1", "Pn", "Qn", "Ls2", "Pz", "Qz", "U", "La3", "Ls3", "V",
+    "S0", "S1", "I1b", "I1c", "I0c", "I0d", "S2", "I1d", "S3", "I0f", "I1f", "T0", "I1g", "I0g", "I1e", "D0", "T1",
+    "I0i", "I0h", "I0e", "P0a", "D1", "R1", "T2", "I1h", "P1a", "R0", "P0b", "I1i", "D2", "Q0a", "Q0b", "T3", "P1b",
+    "R2", "In", "D3", "Q1b", "Q1a", "Iz", "P1c", "P0c", "Q0c", "Ra1", "P1d", "P0e", "Q0d", "R3", "P1e", "Ra0",
+    "Q1c", "Rs1", "G1", "Q1d", "P1f", "P0f", "P0d", "Rs0", "G0", "Ra2", "Ra3", "Q0f", "Rs2", "Q1f", "G2", "Q1e",
+    "P0i", "Rs3", "Q1g", "G3", "Q0g", "Q0h", "P1i", "La1", "P1h", "P0g", "Q0e", "Q1i", "Pn", "La0", "Ls1", "P1g",
+    "Q1h", "Q0i", "P0h", "La2", "Pz", "Qn", "Qz", "Ls2", "Ls0", "La3", "U", "Ls3", "V",
 ]
 
 
@@ -299,22 +294,31 @@
 
     mine = pl.ds(pl.multiple_of((me.y * 4 + me.z) * ROWS, ROWS), ROWS)
     own_rows = pl.ds(pl.multiple_of(me.own * WIDE, WIDE), WIDE)
-    chunk = [slice(c * CHUNK, (c + 1) * CHUNK) for c in range(CHUNKS)]
-    row_sems = CHUNKS * ROW
+    row_sems = max(map(len, SIZES)) * ROW
     planes = 3 * row_sems
-    plane_sems = [[planes], [planes + PLANE, planes + 2 * PLANE], [planes, planes + 3 * PLANE]]
-    ham_sems = [planes + 4 * PLANE, planes + 5 * PLANE]
-    filters_sem, energy_sem = planes + 6 * PLANE, planes + 6 * PLANE + 1
-
-    def row_chunks(buf, send, group):
-        return [Row(cp, me, buf, send, group * row_sems + c * ROW, c * CHUNK) for c in range(CHUNKS)]
+    odd_sems = [planes + i * PLANE for i in range(len(SIZES[0]) // 2)]
+    even_sems = [planes + (len(odd_sems) + i) * PLANE for i in range(len(SIZES[1]) // 2)]
+    ham_first = planes + (len(odd_sems) + len(even_sems)) * PLANE
+    ham_sems = [ham_first, ham_first + PLANE]
+    filters_sem, energy_sem = ham_first + 2 * PLANE, ham_first + 2 * PLANE + 1
+
+    def row_chunks(buf, send, group, sizes):
+        return [
+            Row(cp, me, buf, send, group * row_sems + c * ROW, sum(sizes[:c]), size) for c, size in enumerate(sizes)
+        ]
 
     def drain_rows(buf, send):
         cp.sent(buf.at[:, : 7 * WIDE], send)
 
+    hams = []
+    for i in range(2):
+        piece = tall_piece(hcol, i * (TALL // 2), TALL // 4)
+        hams.append(Plane(cp, me, hcol, piece, TALL // 4, SLIM, 4 + i, ham_sems[i]))
+    ham_tasks = {**hams[0].tasks("H"), **hams[1].tasks("I")}
+
     cp.send(filters, others, 6, filters_sem, me.partner())
     panel = colp.at[0]
-    plane = Plane(cp, me, panel, tall_piece(panel, 0, TALL // 2, 1), TALL // 2, SLIM, 2, plane_sems[0][0])
+    plane = Plane(cp, me, panel, tall_piece(panel, 0, TALL // 2, 1), TALL // 2, SLIM, 2, even_sems[0])
     whole = Row(cp, me, rowp, 0, 0, 0, ROWS)
     first = Product(rowp, panel)
 
@@ -322,12 +326,8 @@
         rowp[:, own_rows] = colp[0, mine]
         whole.start()
 
-    def whole_shared():
-        whole.shared_own()
-        whole.shared()
-
-    tasks = plane.tasks("A")
-    tasks.update(R=whole_start, Ra=whole.arrive, Rs=whole_shared, E=lambda: first.blocks(me, EARLY))
+    tasks = {**plane.tasks("A"), **ham_tasks}
+    tasks.update(R=whole_start, Ra=whole.arrive, Rs=whole.shared, E=lambda: first.blocks(me, EARLY))
     run(tasks, ORDER_A)
     plane.drain()
     cp.arrive(others, filters_sem)
@@ -335,24 +335,28 @@
     for step in range(2):
         drain_rows(rowp, 0)
         panel, after = colp.at[step], colp.at[1 - step]
-        ham_piece = tall_piece(hcol, step * (TALL // 2), TALL // 4)
-        ham = Plane(cp, me, hcol, ham_piece, TALL // 4, SLIM, 4 + step, ham_sems[step])
-        pair = [
-            Plane(cp, me, after, chunk_piece(after, 2 * i), CHUNK, WIDE, 3 - step, plane_sems[step + 1][i])
-            for i in range(2)
-        ]
-        inner, rows, last = row_chunks(srow, 1, 1), row_chunks(rowp, 0, 0), row_chunks(grow, 7, 2)
-        thirds = [Product(srow, panel, c * CHUNK, CHUNK) for c in range(CHUNKS)]
+        sizes = SIZES[step]
+        count = len(sizes)
+        chunk = [slice(sum(sizes[:c]), sum(sizes[: c + 1])) for c in range(count)]
+        sems = odd_sems if step == 0 else even_sems
+        pairs = []
+        for i in range(0, count, 2):
+            piece = chunk_piece(after, chunk[i].start, sizes[i])
+            pairs.append(Plane(cp, me, after, piece, sizes[i], WIDE, 3 - step, sems[i // 2]))
+        inner, rows = row_chunks(srow, 1, 1, sizes), row_chunks(rowp, 0, 0, sizes)
+        last = row_chunks(grow, 7, 2, sizes)
+        thirds = [Product(srow, panel, chunk[c].start, sizes[c]) for c in range(count)]
         own_piece, own_block = after.at[mine], rowp.at[:, own_rows]
         blocks = [filters[step].astype(F32), others[step].astype(F32)]
         keep = [jnp.where(me.zl == 0, m[:, :4], m[:, 4:]) for m in blocks]
         left = jnp.where(me.zl == 0, keep[0], keep[1])
         right = jnp.where(me.zl == 0, keep[1], keep[0])
         early = first.total
-        upper, lower = Product(grow, after, 0, 3 * CHUNK), Product(grow, after, 3 * CHUNK, CHUNK)
+        cut = chunk[-1].start
+        upper, lower = Product(grow, after, 0, cut), Product(grow, after, cut, sizes[-1])
 
         def square_chunk(c):
-            tail = Product(rowp, panel, c * CHUNK, CHUNK)
+            tail = Product(rowp, panel, chunk[c].start, sizes[c])
             tail.total = early[chunk[c]]
             tail.blocks(me, LATE)
             srow[chunk[c], own_rows] = tail.total.astype(BF)
@@ -364,74 +368,68 @@
             thirds[c].tiles(me, 0, 0, 1, 3, 2)
 
         def dens_chunk(c):
-            inner[c].shared_own()
             inner[c].shared()
             thirds[c].tiles(me, 1, 0, 1, 3, 2)
-            mask = jnp.concatenate([mask_row(left, c), mask_row(right, c)], axis=1)
-            dens = (mask * (3.0 * square[chunk[c]] - 2.0 * thirds[c].total)).astype(BF)
-            own_piece[chunk[c]] = dens
-            own_block[chunk[c]] = dens
+            lo = chunk[c].start
+            while lo < chunk[c].stop:
+                hi = min(lo // BS * BS + BS, chunk[c].stop)
+                mask = jnp.concatenate([mask_row(left, lo // BS), mask_row(right, lo // BS)], axis=1)
+                third = thirds[c].total[lo - chunk[c].start : hi - chunk[c].start]
+                dens = (mask * (3.0 * square[lo:hi] - 2.0 * third)).astype(BF)
+                own_piece[lo:hi] = dens
+                own_block[lo:hi] = dens
+                lo = hi
 
         def rows_start(c):
-            if c == CHUNKS - 1:
+            if c == count - 1:
                 drain_rows(srow, 1)
             rows[c].start()
 
-        def rows_shared(c):
-            rows[c].shared_own()
-            rows[c].shared()
-
         def inward(c):
-            part = Product(rowp, hcol, c * CHUNK, CHUNK)
+            part = Product(rowp, hcol, chunk[c].start, sizes[c])
             part.tiles(me, 0, 0, 1, 3, 2)
             part.tiles(me, 1, 0, 1, 3, 2)
             grow[chunk[c], own_rows] = part.total.astype(BF)
             last[c].start()
 
-        def last_shared(c):
-            last[c].shared_own()
-            last[c].shared()
-
-        def give(c):
-            for dk in range(2):
-                k = (me.k + dk) % 2
-                src = etile.at[pl.ds(pl.multiple_of(c * CHUNK + k * OWN, OWN), OWN)]
-                target = me.by(dx=4 - me.x + c, dk=dk)
-
-                def send():
+        def give(lo, hi):
+            for owner in range(lo // OWN, hi // OWN):
+                src = etile.at[owner * OWN : (owner + 1) * OWN]
+                target = me.at(owner // 2, me.y, me.z, owner % 2)
+
+                @pl.when(me.own != owner)
+                def _():
                     cp.send(src, eall.at[:, own_rows], 8, energy_sem, target)
-
-                if dk:
-                    send()
-                else:
-                    pl.when(me.x != c)(send)
 
         def energy_upper():
             for dk in range(2):
                 upper.tiles(me, dk, 0, 1, 3, 2)
-            etile[: 3 * CHUNK] = upper.total.astype(BF)
-            for c in range(3):
-                give(c)
+            etile[:cut] = upper.total.astype(BF)
+            give(0, cut)
 
         def energy_lower():
             for dk in range(2):
                 lower.tiles(me, dk, 0, 1, 3, 2)
-            etile[3 * CHUNK :] = lower.total.astype(BF)
-            give(3)
-
-        tasks = {**ham.tasks("H"), **pair[0].tasks("P"), **pair[1].tasks("Q")}
-        steps = dict(S=square_chunk, T=third_chunk, D=dens_chunk, R=rows_start, Rs=rows_shared, G=inward, Ls=last_shared)
-        for c in range(CHUNKS):
+            etile[cut:] = lower.total.astype(BF)
+            give(cut, ROWS)
+
+        tasks = dict(ham_tasks)
+        for name, pair in zip("PQW", pairs):
+            tasks.update(pair.tasks(name))
+        steps = dict(S=square_chunk, T=third_chunk, D=dens_chunk, R=rows_start, G=inward)
+        for c in range(count):
             tasks.update({name + str(c): functools.partial(f, c) for name, f in steps.items()})
-            tasks.update({"Ra" + str(c): rows[c].arrive, "La" + str(c): last[c].arrive})
+            tasks.update({"Ra" + str(c): rows[c].arrive, "Rs" + str(c): rows[c].shared})
+            tasks.update({"La" + str(c): last[c].arrive, "Ls" + str(c): last[c].shared})
         if step == 0:
             first = Product(rowp, after)
             tasks.update(E=functools.partial(first.blocks, me, EARLY))
         tasks.update(U=energy_upper, V=energy_lower)
         run(tasks, ORDER_B if step == 0 else ORDER_C)
-        cp.sent(after.at[: 60 * CHUNK], 3 - step)
+        cp.sent(after.at[: 15 * ROWS], 3 - step)
+
+    for ham in hams:
         ham.drain()
-
     drain_rows(rowp, 0)
     drain_rows(grow, 7)
     eall[:, own_rows] = etile[pl.ds(pl.multiple_of(me.own * OWN, OWN), OWN)]
@@ -462,6 +460,7 @@
 def body(hamil, guess, pattern, filters, deriv, atom_of_row):
     args = (hamil, guess, pattern.T, filters.transpose(0, 2, 1), deriv, atom_of_row.reshape(1, OWN))
     vmem = pl.BlockSpec(memory_space=pltpu.VMEM)
+    sems = 3 * max(map(len, SIZES)) * ROW + (sum(map(len, SIZES)) // 2 + 2) * PLANE + 2
     return pl.pallas_call(
         kernel,
         out_shape=(
@@ -483,7 +482,7 @@
             pltpu.VMEM(args[3].shape, args[3].dtype),
             pltpu.SemaphoreType.DMA((6,)),
             pltpu.SemaphoreType.DMA((9,)),
-            pltpu.SemaphoreType.DMA((3 * CHUNKS * ROW + 6 * PLANE + 2,)),
+            pltpu.SemaphoreType.DMA((sems,)),
         ],
         compiler_params=pltpu.CompilerParams(
             collective_id=0, has_side_effects=True, vmem_limit_bytes=60 * 1024 * 1024

time: 115 us -> 115 us (level)
  no operation moved by 1% of the time
where the time goes in v6:
time: 115 us; the launch traced here: 114 us
  Pallas kernels  112 us (97%)
  local copies, waits for them, and re-layouts  2.25 us (2%)
    pallas_call x1, Pallas kernels, body(): pl.pallas_call(kernel, out_shape=(jax.ShapeDtypeStruct((OWN, N), BF), jax...  112 us

profile of v6, /device:TPU:1, one launch (start us, length us, event | category | flops | bytes accessed | tf_op | source)
XLA Modules:
  0.0 114.5 jit_solution(3939121473782077810)
XLA Ops:
  0.6 111.6 %shard_map.77 = (bf16[32,4096]{1,0:T(8,128)(2,1)}, f32[3,4]{1,0:T(4,128)}) custom-call(bf16[512,256]{1,0:T(8,128)(2,1)} %hamil_hbm.1, bf16[512,256]{1,0:T(8,128)(2,1)} %guess_hbm.1, s32[4,8]{1,0:T(4,128)} %bitcast.4, s32[2,4,8]{2,1,0:T(4,128)} %bitcast.3, bf16[3,32,4096]{2,1,0:T(8,128)(2,1)} %deriv_hbm.1, s32[1,32]{1,0:T(1,128)} %bitcast.5), custom_call_target="tpu_custom_call" | custom-call | tf_op jit(solution)/shard_map/pallas_call | solution.py:464
  112.2 0.0 copy-start
  112.2 1.7 %copy.10 = bf16[32,4096]{1,0:T(8,128)(2,1)} copy(bf16[32,4096]{1,0:T(8,128)(2,1)} %get-tuple-element.4) | data formatting | bytes 524288
  113.9 0.0 copy-done
  113.9 0.6 copy.11
Async XLA Ops:
  112.2 1.7 %copy-start = (f32[3,4]{1,0:T(4,128)S(1)}, f32[3,4]{1,0:T(4,128)}, u32[]{:S(2)}) copy-start(f32[3,4]{1,0:T(4,128)} %get-tuple-element.5) | copy-start | bytes 148

commit v7 on v6

--- a/solution.py
+++ b/solution.py
@@ -235,24 +235,24 @@
 
 
 ORDER_A = [
-    "A0a", "A1a", "A0b", "A1b", "A0c", "A1c", "R", "A1d", "A0d", "A1f", "A0f", "A1h", "A1g", "A0h", "A0g", "A1e",
-    "A1i", "A0e", "A0i", "H1a", "H0a", "H1b", "Ra", "Rs", "An", "H0b", "E", "Az",
+    "A1a", "A0a", "A1b", "A0b", "A1c", "A0c", "A1d", "A0d", "R", "A0f", "A1f", "A0e", "A0h", "A1e", "A1h", "A0g",
+    "A1g", "A0i", "A1i", "An", "H1a", "Ra", "H0a", "H0b", "Rs", "H1b", "E", "Az",
 ]
 ORDER_B = [
-    "S0", "S1", "H1c", "H0c", "H1d", "H0d", "S2", "S3", "H0e", "H1e", "H0f", "H1f", "H1g", "T0", "H0h", "H0g", "D0",
-    "P0b", "P0a", "H1h", "T1", "H0i", "H1i", "D1", "P1a", "P1b", "T2", "P0c", "R0", "P0d", "R1", "D2", "Q0a", "T3",
-    "P1c", "P1d", "D3", "Q1a", "R3", "Q0c", "Q0d", "Hn", "Q1b", "P1f", "Q1c", "P0f", "P1e", "Ra0", "Q1d", "Q0b",
-    "Q0f", "P0e", "Q1e", "P1g", "R2", "Q1f", "Q0h", "P1i", "P0g", "P1h", "P0h", "P0i", "Q1h", "Q1g", "Q0g", "Ra3",
-    "Rs3", "Q0i", "Hz", "Ra1", "Q0e", "Q1i", "Ra2", "Pn", "I0a", "Rs0", "Qn", "I1a", "Rs2", "Rs1", "Pz", "E", "I0b",
-    "Qz",
+    "S0", "H1c", "H0c", "H0d", "S1", "H1d", "S2", "S3", "H1f", "H1g", "T0", "H1h", "H0e", "H0g", "H0f", "D0", "P0a",
+    "T1", "H1i", "H1e", "P0b", "D1", "P1a", "T2", "P1b", "P0c", "P0d", "D2", "Q0a", "Hn", "T3", "P1c", "P1d", "Q0b",
+    "R0", "D3", "R3", "Q1a", "Q0c", "P0f", "Q1b", "H0h", "H0i", "P1f", "R1", "R2", "Q1c", "Q1d", "Q0f", "Q0d",
+    "P0g", "Q0e", "P0h", "P1i", "P1e", "P0i", "Q1f", "P0e", "Ra0", "Ra1", "Q1h", "P1g", "Hz", "Q0h", "P1h", "Ra3",
+    "Q0g", "Rs0", "Q1g", "Q0i", "I1a", "Q1e", "Pn", "Q1i", "Ra2", "Qn", "I0a", "Pz", "Rs3", "Rs1", "Rs2", "I0b",
+    "I1b", "E", "Qz",
 ]
 ORDER_C = [
-    "S0", "S1", "I1b", "I1c", "I0c", "I0d", "S2", "I1d", "S3", "I0f", "I1f", "T0", "I1g", "I0g", "I1e", "D0", "T1",
-    "I0i", "I0h", "I0e", "P0a", "D1", "R1", "T2", "I1h", "P1a", "R0", "P0b", "I1i", "D2", "Q0a", "Q0b", "T3", "P1b",
-    "R2", "In", "D3", "Q1b", "Q1a", "Iz", "P1c", "P0c", "Q0c", "Ra1", "P1d", "P0e", "Q0d", "R3", "P1e", "Ra0",
-    "Q1c", "Rs1", "G1", "Q1d", "P1f", "P0f", "P0d", "Rs0", "G0", "Ra2", "Ra3", "Q0f", "Rs2", "Q1f", "G2", "Q1e",
-    "P0i", "Rs3", "Q1g", "G3", "Q0g", "Q0h", "P1i", "La1", "P1h", "P0g", "Q0e", "Q1i", "Pn", "La0", "Ls1", "P1g",
-    "Q1h", "Q0i", "P0h", "La2", "Pz", "Qn", "Qz", "Ls2", "Ls0", "La3", "U", "Ls3", "V",
+    "S0", "I1c", "I0c", "I1d", "I0d", "S1", "I1f", "S2", "I0f", "T0", "I0e", "I1e", "I1g", "I0g", "S3", "I0h", "D0",
+    "I1h", "P0a", "P0b", "T1", "I0i", "D1", "R1", "P1a", "I1i", "T2", "P1b", "R0", "D2", "Q0b", "Q0a", "R2", "T3",
+    "P1c", "P1d", "P0c", "In", "D3", "Q1a", "P0d", "Q1b", "R3", "Ra1", "Q0c", "Rs1", "Iz", "G1", "Q1c", "P1h",
+    "Ra0", "Q0d", "P1f", "Rs0", "Q1d", "G0", "Ra2", "P0f", "Q1f", "Q0f", "P0e", "Q0h", "Rs2", "Q0g", "Q1e", "P1g",
+    "Ra3", "Q0e", "P0g", "P1e", "G2", "Q1g", "Q1h", "P0i", "P1i", "Rs3", "G3", "La1", "Q1i", "Q0i", "P0h", "La0",
+    "Qn", "La2", "Ls1", "Ls0", "Pn", "Qz", "Pz", "Ls2", "U", "La3", "Ls3", "V",
 ]
 
 

time: 115 us -> 114 us (level)
  no operation moved by 1% of the time
where the time goes in v7:
time: 114 us
  Pallas kernels  111 us (97%)
  local copies, waits for them, and re-layouts  2.25 us (2%)
    pallas_call x1, Pallas kernels, body(): pl.pallas_call(kernel, out_shape=(jax.ShapeDtypeStruct((OWN, N), BF), jax...  111 us

profile of v7, /device:TPU:1, one launch (start us, length us, event | category | flops | bytes accessed | tf_op | source)
XLA Modules:
  0.0 113.7 jit_solution(7413836172861140055)
XLA Ops:
  0.6 110.8 %shard_map.77 = (bf16[32,4096]{1,0:T(8,128)(2,1)}, f32[3,4]{1,0:T(4,128)}) custom-call(bf16[512,256]{1,0:T(8,128)(2,1)} %hamil_hbm.1, bf16[512,256]{1,0:T(8,128)(2,1)} %guess_hbm.1, s32[4,8]{1,0:T(4,128)} %bitcast.4, s32[2,4,8]{2,1,0:T(4,128)} %bitcast.3, bf16[3,32,4096]{2,1,0:T(8,128)(2,1)} %deriv_hbm.1, s32[1,32]{1,0:T(1,128)} %bitcast.5), custom_call_target="tpu_custom_call" | custom-call | tf_op jit(solution)/shard_map/pallas_call | solution.py:464
  111.4 0.0 copy-start
  111.4 1.7 %copy.10 = bf16[32,4096]{1,0:T(8,128)(2,1)} copy(bf16[32,4096]{1,0:T(8,128)(2,1)} %get-tuple-element.4) | data formatting | bytes 524288
  113.1 0.0 copy-done
  113.1 0.6 copy.11
Async XLA Ops:
  111.4 1.7 %copy-start = (f32[3,4]{1,0:T(4,128)S(1)}, f32[3,4]{1,0:T(4,128)}, u32[]{:S(2)}) copy-start(f32[3,4]{1,0:T(4,128)} %get-tuple-element.5) | copy-start | bytes 148

commit v8 on v7

--- a/solution.py
+++ b/solution.py
@@ -249,10 +249,10 @@
 ORDER_C = [
     "S0", "I1c", "I0c", "I1d", "I0d", "S1", "I1f", "S2", "I0f", "T0", "I0e", "I1e", "I1g", "I0g", "S3", "I0h", "D0",
     "I1h", "P0a", "P0b", "T1", "I0i", "D1", "R1", "P1a", "I1i", "T2", "P1b", "R0", "D2", "Q0b", "Q0a", "R2", "T3",
-    "P1c", "P1d", "P0c", "In", "D3", "Q1a", "P0d", "Q1b", "R3", "Ra1", "Q0c", "Rs1", "Iz", "G1", "Q1c", "P1h",
-    "Ra0", "Q0d", "P1f", "Rs0", "Q1d", "G0", "Ra2", "P0f", "Q1f", "Q0f", "P0e", "Q0h", "Rs2", "Q0g", "Q1e", "P1g",
-    "Ra3", "Q0e", "P0g", "P1e", "G2", "Q1g", "Q1h", "P0i", "P1i", "Rs3", "G3", "La1", "Q1i", "Q0i", "P0h", "La0",
-    "Qn", "La2", "Ls1", "Ls0", "Pn", "Qz", "Pz", "Ls2", "U", "La3", "Ls3", "V",
+    "P1c", "P1d", "P0c", "In", "D3", "Q1a", "P0d", "Q1b", "R3", "Ra1", "Q0c", "Rs1", "Iz", "Go1", "G1", "Q1c",
+    "P1h", "Ra0", "Q0d", "P1f", "Go0", "Rs0", "Q1d", "G0", "Ra2", "P0f", "Q1f", "Q0f", "P0e", "Q0h", "Go2", "Rs2",
+    "Q0g", "Q1e", "P1g", "Ra3", "Q0e", "P0g", "P1e", "G2", "Q1g", "Q1h", "P0i", "P1i", "Go3", "Rs3", "G3", "La1",
+    "Q1i", "Q0i", "P0h", "La0", "Qn", "La2", "Ls1", "Ls0", "Pn", "Qz", "Pz", "Ls2", "U", "La3", "Vo", "Ls3", "V",
 ]
 
 
@@ -346,6 +346,7 @@
         inner, rows = row_chunks(srow, 1, 1, sizes), row_chunks(rowp, 0, 0, sizes)
         last = row_chunks(grow, 7, 2, sizes)
         thirds = [Product(srow, panel, chunk[c].start, sizes[c]) for c in range(count)]
+        inwards = [Product(rowp, hcol, chunk[c].start, sizes[c]) for c in range(count)]
         own_piece, own_block = after.at[mine], rowp.at[:, own_rows]
         blocks = [filters[step].astype(F32), others[step].astype(F32)]
         keep = [jnp.where(me.zl == 0, m[:, :4], m[:, 4:]) for m in blocks]
@@ -385,11 +386,12 @@
                 drain_rows(srow, 1)
             rows[c].start()
 
+        def inward_own(c):
+            inwards[c].tiles(me, 0, 0, 1, 3, 2)
+
         def inward(c):
-            part = Product(rowp, hcol, chunk[c].start, sizes[c])
-            part.tiles(me, 0, 0, 1, 3, 2)
-            part.tiles(me, 1, 0, 1, 3, 2)
-            grow[chunk[c], own_rows] = part.total.astype(BF)
+            inwards[c].tiles(me, 1, 0, 1, 3, 2)
+            grow[chunk[c], own_rows] = inwards[c].total.astype(BF)
             last[c].start()
 
         def give(lo, hi):
@@ -407,16 +409,18 @@
             etile[:cut] = upper.total.astype(BF)
             give(0, cut)
 
+        def energy_lower_own():
+            lower.tiles(me, 0, 0, 1, 3, 2)
+
         def energy_lower():
-            for dk in range(2):
-                lower.tiles(me, dk, 0, 1, 3, 2)
+            lower.tiles(me, 1, 0, 1, 3, 2)
             etile[cut:] = lower.total.astype(BF)
             give(cut, ROWS)
 
         tasks = dict(ham_tasks)
         for name, pair in zip("PQW", pairs):
             tasks.update(pair.tasks(name))
-        steps = dict(S=square_chunk, T=third_chunk, D=dens_chunk, R=rows_start, G=inward)
+        steps = dict(S=square_chunk, T=third_chunk, D=dens_chunk, R=rows_start, Go=inward_own, G=inward)
         for c in range(count):
             tasks.update({name + str(c): functools.partial(f, c) for name, f in steps.items()})
             tasks.update({"Ra" + str(c): rows[c].arrive, "Rs" + str(c): rows[c].shared})
@@ -424,7 +428,7 @@
         if step == 0:
             first = Product(rowp, after)
             tasks.update(E=functools.partial(first.blocks, me, EARLY))
-        tasks.update(U=energy_upper, V=energy_lower)
+        tasks.update(U=energy_upper, Vo=energy_lower_own, V=energy_lower)
         run(tasks, ORDER_B if step == 0 else ORDER_C)
         cp.sent(after.at[: 15 * ROWS], 3 - step)
 

time: 114 us -> 114 us (level)
  no operation moved by 1% of the time
where the time goes in v8:
time: 114 us
  Pallas kernels  111 us (97%)
  local copies, waits for them, and re-layouts  2.25 us (2%)
    pallas_call x1, Pallas kernels, body(): pl.pallas_call(kernel, out_shape=(jax.ShapeDtypeStruct((OWN, N), BF), jax...  111 us

profile of v8, /device:TPU:1, one launch (start us, length us, event | category | flops | bytes accessed | tf_op | source)
XLA Modules:
  0.0 113.7 jit_solution(12183334797466998050)
XLA Ops:
  0.6 110.8 %shard_map.77 = (bf16[32,4096]{1,0:T(8,128)(2,1)}, f32[3,4]{1,0:T(4,128)}) custom-call(bf16[512,256]{1,0:T(8,128)(2,1)} %hamil_hbm.1, bf16[512,256]{1,0:T(8,128)(2,1)} %guess_hbm.1, s32[4,8]{1,0:T(4,128)} %bitcast.4, s32[2,4,8]{2,1,0:T(4,128)} %bitcast.3, bf16[3,32,4096]{2,1,0:T(8,128)(2,1)} %deriv_hbm.1, s32[1,32]{1,0:T(1,128)} %bitcast.5), custom_call_target="tpu_custom_call" | custom-call | tf_op jit(solution)/shard_map/pallas_call | solution.py:468
  111.4 0.0 copy-start
  111.4 1.7 %copy.10 = bf16[32,4096]{1,0:T(8,128)(2,1)} copy(bf16[32,4096]{1,0:T(8,128)(2,1)} %get-tuple-element.4) | data formatting | bytes 524288
  113.1 0.0 copy-done
  113.1 0.6 copy.11
Async XLA Ops:
  111.4 1.7 %copy-start = (f32[3,4]{1,0:T(4,128)S(1)}, f32[3,4]{1,0:T(4,128)}, u32[]{:S(2)}) copy-start(f32[3,4]{1,0:T(4,128)} %get-tuple-element.5) | copy-start | bytes 148

commit v9 on v8

--- a/solution.py
+++ b/solution.py
@@ -449,15 +449,10 @@
                 :, b * WIDE + zl * SLIM : b * WIDE + (zl + 1) * SLIM
             ]
     wide = energy_out[...].astype(F32)
-    line = lax.broadcasted_iota(jnp.int32, (3, ATOM_DEV), 0)
-    lane = lax.broadcasted_iota(jnp.int32, (3, ATOM_DEV), 1)
-    forces = jnp.zeros((3, ATOM_DEV), F32)
+    lane = lax.broadcasted_iota(jnp.int32, (OWN, ATOM_DEV), 1).astype(F32)
     for axis in range(3):
         per_row = jnp.sum(deriv[axis].astype(F32) * wide, axis=1, keepdims=True)
-        for atom in range(ATOM_DEV):
-            force = jnp.sum(jnp.where(atom_of == atom, per_row, 0.0))
-            forces = jnp.where((line == axis) & (lane == atom), force, forces)
-    forces_out[...] = forces
+        forces_out[axis : axis + 1] = jnp.sum(jnp.where(atom_of == lane, per_row, 0.0), axis=0, keepdims=True)
     cp.sent(eall.at[:, : 7 * WIDE], 8)
 
 

time: 114 us -> 114 us (level)
  no operation moved by 1% of the time
where the time goes in v9:
time: 114 us
  Pallas kernels  111 us (97%)
  local copies, waits for them, and re-layouts  2.25 us (2%)
    pallas_call x1, Pallas kernels, body(): pl.pallas_call(kernel, out_shape=(jax.ShapeDtypeStruct((OWN, N), BF), jax...  111 us

profile of v9, /device:TPU:1, one launch (start us, length us, event | category | flops | bytes accessed | tf_op | source)
XLA Modules:
  0.0 113.6 jit_solution(79803820265935490)
XLA Ops:
  0.6 110.7 %shard_map.77 = (bf16[32,4096]{1,0:T(8,128)(2,1)}, f32[3,4]{1,0:T(4,128)}) custom-call(bf16[512,256]{1,0:T(8,128)(2,1)} %hamil_hbm.1, bf16[512,256]{1,0:T(8,128)(2,1)} %guess_hbm.1, s32[4,8]{1,0:T(4,128)} %bitcast.4, s32[2,4,8]{2,1,0:T(4,128)} %bitcast.3, bf16[3,32,4096]{2,1,0:T(8,128)(2,1)} %deriv_hbm.1, s32[1,32]{1,0:T(1,128)} %bitcast.5), custom_call_target="tpu_custom_call" | custom-call | tf_op jit(solution)/shard_map/pallas_call | solution.py:463
  111.3 0.0 copy-start
  111.3 1.7 %copy.10 = bf16[32,4096]{1,0:T(8,128)(2,1)} copy(bf16[32,4096]{1,0:T(8,128)(2,1)} %get-tuple-element.4) | data formatting | bytes 524288
  113.0 0.0 copy-done
  113.0 0.6 copy.11
Async XLA Ops:
  111.3 1.7 %copy-start = (f32[3,4]{1,0:T(4,128)S(1)}, f32[3,4]{1,0:T(4,128)}, u32[]{:S(2)}) copy-start(f32[3,4]{1,0:T(4,128)} %get-tuple-element.5) | copy-start | bytes 148
